TPU v7x, 32 devices: a whole 2x2x4 slice. The times are simulated.
32 devices in a mesh: batch: 16 (over z, x, core), seq: 2 (over y).
Axes of the slice: x: 2, y: 2, z: 4, core: 2. Of those that a mesh axis runs over, the one named last changes fastest.
Arguments:
- inputs: bfloat16 [4, 32, 1024, 1280], P(None, 'batch', 'seq'), may hold values from -6 to 6
- cotangent: bfloat16 [4, 32, 1024, 1280], P(None, 'batch', 'seq'), may hold values from -6 to 6
- lengths: int32 [4, 32], P(None, 'batch'), may hold values from 30 to 1024, as said below
- w_first: bfloat16 [1280, 640], P(('batch', 'seq')), may hold values from -0.15625 to 0.15625
- tap_weights: bfloat16 [5, 640, 640], P(None, 'batch', 'seq'), may hold values from -0.109375 to 0.109375
- w_last: bfloat16 [640, 1280], P(None, ('batch', 'seq')), may hold values from -0.25 to 0.25
- norm_gain: bfloat16 [2560], P(('batch', 'seq')), may hold values from 0.5 to 1.5
- shift_params: bfloat16 [2, 2560], P(None, ('batch', 'seq')), may hold values from -2 to 2
Outputs:
- outputs: bfloat16 [4, 32, 1024, 1280], P(None, 'batch', 'seq')
- input_grad: bfloat16 [4, 32, 1024, 1280], P(None, 'batch', 'seq')
- grad_first: float32 [1280, 640], P(('batch', 'seq'))
- grad_taps: float32 [5, 640, 640], P(None, 'batch', 'seq')
- grad_last: float32 [640, 1280], P(None, ('batch', 'seq'))
- grad_gain: float32 [2560], P(('batch', 'seq'))
- grad_shift: float32 [2, 2560], P(None, ('batch', 'seq'))
Inputs may be any that keep to these rules, and one draw needn't show every extreme that they name: `lengths`: for each aligned block of 2 sequences, at least one of the 8 entries that the block holds over all micro-batches has length 1024; the others may be shorter.
All inputs are finite; a program needn't handle non-finite values.
Results may differ from a plain program's by a relative error of at most 0.0068.
Values may be sent and summed in bfloat16 or wider, within the bound.
No kernel may reach another device: no remote copies, remote signals or barrier semaphores. Data moves between devices by JAX's collectives and lax.ppermute only.
A program may use at most 256 MiB of HBM per device.

v0:
```python
import jax
import jax.numpy as jnp
from jax import lax
from jax.sharding import PartitionSpec as P

DILATION_STEP = 128


def shifted(value, axis, steps):
    count = lax.axis_size(axis)
    initial, last = (max(0, -steps), min(count, count - steps))
    return lax.ppermute(value, axis, [(source, source + steps) for source in range(initial, last)])


def norm_act(values, gain_row, shift_row):
    row_mean = jnp.mean(values, axis=-1, keepdims=True)
    centered = values - row_mean
    variance = jnp.mean(centered * centered, axis=-1, keepdims=True)
    return jax.nn.gelu(
        centered * lax.rsqrt(variance + 1e-05) * gain_row + shift_row, approximate=False
    )


def gather_weights(w_first, tap_weights, w_last, norm_gain, shift_params, n_batch, n_seq):
    pieces = (
        lax.all_gather(w_first, ("batch", "seq"), axis=0, tiled=True),
        lax.all_gather(tap_weights[None], ("batch", "seq"), axis=0, tiled=True),
        lax.all_gather(w_last, ("batch", "seq"), axis=1, tiled=True),
        lax.all_gather(norm_gain, ("batch", "seq"), axis=0, tiled=True),
        lax.all_gather(shift_params, ("batch", "seq"), axis=1, tiled=True),
    )
    kernel_taps, rows_part, cols_part = tap_weights.shape
    stacked = pieces[1].reshape(n_batch, n_seq, kernel_taps, rows_part, cols_part)
    taps_full = stacked.transpose(2, 0, 3, 1, 4).reshape(
        kernel_taps, n_batch * rows_part, n_seq * cols_part
    )
    return (
        pieces[0],
        taps_full,
        pieces[2],
        pieces[3].astype(jnp.float32),
        pieces[4].astype(jnp.float32),
    )


def scatter_grads(grad_parts, n_batch, n_seq):
    grad_first, grad_taps, grad_last, grad_gain, grad_shift = grad_parts
    kernel_taps, rows_all, cols_all = grad_taps.shape
    arranged = grad_taps.reshape(
        kernel_taps, n_batch, rows_all // n_batch, n_seq, cols_all // n_seq
    )
    arranged = arranged.transpose(1, 3, 0, 2, 4).reshape(
        n_batch * n_seq, kernel_taps, rows_all // n_batch, cols_all // n_seq
    )
    pieces = (
        lax.psum_scatter(grad_first, ("batch", "seq"), scatter_dimension=0, tiled=True),
        lax.psum_scatter(arranged, ("batch", "seq"), scatter_dimension=0, tiled=True),
        lax.psum_scatter(grad_last, ("batch", "seq"), scatter_dimension=1, tiled=True),
        lax.psum_scatter(grad_gain, ("batch", "seq"), scatter_dimension=0, tiled=True),
        lax.psum_scatter(grad_shift, ("batch", "seq"), scatter_dimension=1, tiled=True),
    )
    return (pieces[0], pieces[1][0], pieces[2], pieces[3], pieces[4])


def forward_mover(rows, shift_by):
    return shifted(rows, "seq", shift_by)


def backward_mover(rows, shift_by):
    return shifted(rows, "seq", shift_by)


def take_rows(rows, offset, mover):
    span_rows = rows.shape[1]
    whole_hops = offset // span_rows
    remainder = offset % span_rows

    def from_peer(hop_count):
        if hop_count == 0:
            return rows
        return mover(rows, -hop_count)

    if remainder == 0:
        return from_peer(whole_hops)
    return jnp.concatenate(
        [from_peer(whole_hops)[:, remainder:], from_peer(whole_hops + 1)[:, :remainder]], axis=1
    )


def micro_step(rows_bf, cot_bf, seq_lengths, weights_full):
    w_first, taps_full, w_last, gains, shifts = weights_full
    count_seq, span_rows, model_width = rows_bf.shape
    inner_width = w_first.shape[1]
    kernel_taps = taps_full.shape[0]
    cut_two = model_width + inner_width
    position = lax.axis_index("seq") * span_rows + jnp.arange(span_rows, dtype=jnp.int32)
    live_mask = (position[None, :] < seq_lengths[:, None]).astype(jnp.float32)[:, :, None]
    rows_in = rows_bf.astype(jnp.float32)
    act_first, pull_first = jax.vjp(norm_act, rows_in, gains[:model_width], shifts[0, :model_width])
    act_first = act_first.astype(jnp.bfloat16)
    mid_first = (
        jnp.einsum("sci,io->sco", act_first, w_first, preferred_element_type=jnp.float32)
        + shifts[1, model_width:cut_two]
    )

    def masked_act(values, gain_row, shift_row):
        return norm_act(values, gain_row, shift_row) * live_mask

    act_second, pull_second = jax.vjp(
        masked_act, mid_first, gains[model_width:cut_two], shifts[0, model_width:cut_two]
    )
    act_second = act_second.astype(jnp.bfloat16)
    tap_offsets = [
        (tap_position - kernel_taps // 2) * DILATION_STEP for tap_position in range(kernel_taps)
    ]
    tap_stack = jnp.concatenate(
        [take_rows(act_second, offset, forward_mover) for offset in tap_offsets], axis=2
    )
    taps_flat = taps_full.reshape(kernel_taps * inner_width, inner_width)
    mid_second = (
        jnp.einsum("scj,jo->sco", tap_stack, taps_flat, preferred_element_type=jnp.float32)
        + shifts[1, cut_two:]
    )
    act_third, pull_third = jax.vjp(norm_act, mid_second, gains[cut_two:], shifts[0, cut_two:])
    act_third = act_third.astype(jnp.bfloat16)
    branch = (
        jnp.einsum("sci,io->sco", act_third, w_last, preferred_element_type=jnp.float32)
        + shifts[1, :model_width]
    )
    result = (rows_in + live_mask * branch).astype(jnp.bfloat16)
    cot_rows = cot_bf.astype(jnp.float32)
    grad_branch = (live_mask * cot_rows).astype(jnp.bfloat16)
    bias_last = jnp.sum(grad_branch.astype(jnp.float32), axis=(0, 1))
    grad_last = jnp.einsum(
        "sci,sco->io", act_third, grad_branch, preferred_element_type=jnp.float32
    )
    grad_act_third = jnp.einsum(
        "sco,io->sci", grad_branch, w_last, preferred_element_type=jnp.float32
    )
    grad_mid_second, gain_third, shift_third = pull_third(grad_act_third)
    grad_mid_second = grad_mid_second.astype(jnp.bfloat16)
    bias_second = jnp.sum(grad_mid_second.astype(jnp.float32), axis=(0, 1))
    grad_taps = jnp.einsum(
        "scj,sco->jo", tap_stack, grad_mid_second, preferred_element_type=jnp.float32
    )
    grad_taps = grad_taps.reshape(kernel_taps, inner_width, inner_width)
    back_stack = jnp.stack(
        [take_rows(grad_mid_second, -offset, backward_mover) for offset in tap_offsets], axis=2
    )
    grad_act_second = jnp.einsum(
        "scko,kio->sci", back_stack, taps_full, preferred_element_type=jnp.float32
    )
    grad_mid_first, gain_second, shift_second = pull_second(grad_act_second)
    grad_mid_first = grad_mid_first.astype(jnp.bfloat16)
    bias_first = jnp.sum(grad_mid_first.astype(jnp.float32), axis=(0, 1))
    grad_first = jnp.einsum(
        "sci,sco->io", act_first, grad_mid_first, preferred_element_type=jnp.float32
    )
    grad_act_first = jnp.einsum(
        "sco,io->sci", grad_mid_first, w_first, preferred_element_type=jnp.float32
    )
    grad_rows, gain_first, shift_first = pull_first(grad_act_first)
    input_grad = (cot_rows + grad_rows).astype(jnp.bfloat16)
    grad_gain = jnp.concatenate([gain_first, gain_second, gain_third])
    grad_shift = jnp.stack(
        [
            jnp.concatenate([shift_first, shift_second, shift_third]),
            jnp.concatenate([bias_last, bias_first, bias_second]),
        ]
    )
    return (result, input_grad, (grad_first, grad_taps, grad_last, grad_gain, grad_shift))


def shards(inputs, cotangent, lengths, w_first, tap_weights, w_last, norm_gain, shift_params):
    n_batch = lax.axis_size("batch")
    n_seq = lax.axis_size("seq")
    micro_count = inputs.shape[0]
    results = []
    in_grads = []
    totals = None
    for batch_step in range(micro_count):
        weights_full = gather_weights(
            w_first, tap_weights, w_last, norm_gain, shift_params, n_batch, n_seq
        )
        result, input_grad, grad_parts = micro_step(
            inputs[batch_step], cotangent[batch_step], lengths[batch_step], weights_full
        )
        shares = scatter_grads(grad_parts, n_batch, n_seq)
        totals = (
            shares
            if totals is None
            else tuple((total + share for total, share in zip(totals, shares)))
        )
        results.append(result)
        in_grads.append(input_grad)
    return (
        jnp.stack(results),
        jnp.stack(in_grads),
        totals[0],
        totals[1],
        totals[2],
        totals[3],
        totals[4],
    )


def solution(mesh):
    placed = (
        P(None, "batch", "seq", None),
        P(None, "batch", "seq", None),
        P(None, "batch"),
        P(("batch", "seq"), None),
        P(None, "batch", "seq"),
        P(None, ("batch", "seq")),
        P(("batch", "seq")),
        P(None, ("batch", "seq")),
    )
    return jax.shard_map(
        shards,
        mesh=mesh,
        in_specs=placed,
        out_specs=(
            P(None, "batch", "seq", None),
            P(None, "batch", "seq", None),
            P(("batch", "seq"), None),
            P(None, "batch", "seq"),
            P(None, ("batch", "seq")),
            P(("batch", "seq")),
            P(None, ("batch", "seq")),
        ),
        check_vma=False,
    )
```

profile of v0, /device:TPU:0, one launch (start us, length us, event | category | flops | bytes accessed | tf_op | source)
XLA Modules:
  0.0 1325.1 jit_solution(624106578437541966)
XLA Ops:
  9.6 42.2 %all-reduce = bf16[2560]{0:T(1024)(128)(2,1)S(1)} all-reduce(bf16[2560]{0:T(1024)(128)(2,1)S(1)} %dynamic-update-slice), channel_id=1, replica_groups=mesh['batch'=16,'seq'=2] {'batch','seq'}, use_global_device_ids=true, to_apply=%add | all-reduce | flops 2560 | bytes 10240
  51.8 65.7 %all-gather.1 = bf16[32,80,2]{1,2,0:T(2,128)(2,1)S(1)} all-gather(bf16[1,80,2]{1,2,0:T(2,128)(2,1)} %bitcast.557), channel_id=1, replica_groups=mesh['batch'=16,'seq'=2] {'batch','seq'}, dimensions={0}, use_global_device_ids=true | all-gather | bytes 10560 | tf_op jit(solution)/shard_map/all_gather | solution.py:30
  127.4 14.1 %multiply_convert_fusion.2 = (bf16[2,512,1280]{2,1,0:T(8,128)(2,1)}, f32[2,512,1280]{2,1,0:T(8,128)}) fusion(f32[2,512]{1,0:T(2,128)S(1)} %fusion.237, f32[2,512]{1,0:T(2,128)S(1)} %get-tuple-element.209, f32[1280]{0:T(1024)S(1)} %get-tuple-element.71, f32[1280]{0:T(1024)S(1)} %slice.367, bf16[4,2,512,1280]{3,2,1,0:T(8,128)(2,1)S(1)} %copy-done), kind=kLoop, calls=%fused_computation.137 | loop fusion | flops 91750400 | bytes 10504192 | tf_op jit(solution)/shard_map/convert_element_type | solution.py:100
  161.3 21.1 %collective-permute-done.2 = bf16[2,512,640]{2,1,0:T(8,128)(2,1)} collective-permute-done((bf16[2,512,640]{2,1,0:T(8,128)(2,1)}, bf16[2,512,640]{2,1,0:T(8,128)(2,1)}, u32[]{:S(2)}, u32[]{:S(2)}) %collective-permute-start.2) | collective-permute-done | bytes 1310752 | tf_op jit(solution)/shard_map/ppermute | solution.py:12
  197.1 8.6 copy.99
  205.7 10.5 reshape.578
  216.2 8.9 add_reduce_fusion.4
  226.6 19.2 %multiply_convert_fusion.8 = (bf16[2,512,640]{2,1,0:T(8,128)(2,1)}, f32[2,512,640]{2,1,0:T(8,128)}) fusion(f32[2,512]{1,0:T(2,128)S(1)} %fusion.239, f32[640]{0:T(1024)S(1)} %get-tuple-element.72, f32[640]{0:T(1024)S(1)} %get-tuple-element.184, f32[2,512]{1,0:T(2,128)S(1)} %broadcast_multiply_fusion.4, f32[2,512,640]{2,1,0:T(8,128)S(1)} %get-tuple-element.193, ...), kind=kLoop, calls=%fused_computation.324 | loop fusion | flops 45875200 | bytes 6569472 | tf_op jit(solution)/shard_map/convert_element_type | solution.py:125
  270.7 10.5 reshape.580
  298.6 14.3 %fusion.250 = (f32[640]{0:T(1024)S(1)}, f32[2,512]{1,0:T(2,128)S(1)}, f32[2,512,640]{2,1,0:T(8,128)S(1)}) fusion(f32[640]{0:T(1024)S(1)} %get-tuple-element.185, f32[2,512]{1,0:T(2,128)S(1)} %broadcast_multiply_fusion.5, f32[2,512,640]{2,1,0:T(8,128)S(1)} %get-tuple-element.191, f32[640]{0:T(1024)S(1)} %get-tuple-element.75, ...), kind=kOutput, calls=%fused_computation.590 | convolution fusion | flops 4247386624 | bytes 15919104 | tf_op jit(solution)/shard_map/scko,kio->sci/dot_general | solution.py:150
  316.4 8.4 fusion.56
  325.5 40.5 %multiply_convert_fusion = (bf16[2,512,1280]{2,1,0:T(8,128)(2,1)S(1)}, f32[2,512,1280]{2,1,0:T(8,128)}, bf16[2,512,1280]{2,1,0:T(8,128)(2,1)S(1)}, f32[2,512,128...) fusion(f32[2,512]{1,0:T(2,128)S(1)} %fusion.243, f32[2,512]{1,0:T(2,128)S(1)} %get-tuple-element.207, ...), kind=kLoop, calls=%fused_computation.113 | loop fusion | flops 275251200 | bytes 31492096 | tf_op jit(solution)/shard_map/convert_element_type | solution.py:100
  375.0 20.0 %multiply_convert_fusion.5 = (bf16[2,512,640]{2,1,0:T(8,128)(2,1)S(1)}, bf16[2,512,640]{2,1,0:T(8,128)(2,1)S(1)}, bf16[2,512,640]{2,1,0:T(8,128)(2,1)S(1)}) fusion(f32[2,512]{1,0:T(2,128)S(1)} %get-tuple-element.186, f32[2,512]{1,0:T(2,128)S(1)} %fusion.244, f32[640]{0:T(1024)S(1)} %get-tuple-element.74, f32[640]{0:T(1024)S(1)} %get-tuple-element.185, ...), kind=kLoop, calls=%fused_computation.279 | loop fusion | flops 139591680 | bytes 11841024 | tf_op jit(solution)/shard_map/convert_element_type | solution.py:112
  411.1 47.3 %collective-permute-done.4 = bf16[2,512,640]{2,1,0:T(8,128)(2,1)S(1)} collective-permute-done((bf16[2,512,640]{2,1,0:T(8,128)(2,1)S(1)}, bf16[2,512,640]{2,1,0:T(8,128)(2,1)S(1)}, u32[]{:S(2)}, u32[]{:S(2)}) %collective-permute-start.4) | collective-permute-done | bytes 1310752 | tf_op jit(solution)/shard_map/ppermute | solution.py:12
  459.8 19.9 %collective-permute-done = bf16[2,512,640]{2,1,0:T(8,128)(2,1)S(1)} collective-permute-done((bf16[2,512,640]{2,1,0:T(8,128)(2,1)S(1)}, bf16[2,512,640]{2,1,0:T(8,128)(2,1)S(1)}, u32[]{:S(2)}, u32[]{:S(2)}) %collective-permute-start) | collective-permute-done | bytes 1310752 | tf_op jit(solution)/shard_map/ppermute | solution.py:12
  525.9 14.2 %multiply_convert_fusion.10 = (bf16[2,512,640]{2,1,0:T(8,128)(2,1)}, f32[2,512,640]{2,1,0:T(8,128)}, bf16[2,512,640]{2,1,0:T(8,128)(2,1)}, f32[2,512,640]{2,1,0:T(8,128)S(1)}) fusion(f32[640]{0:T(1024)S(1)} %get-tuple-element.72, f32[640]{0:T(1024)S(1)} %get-tuple-element.184, f32[2,512]{1,0:T(2,128)S(1)} %fusion.236, ...), kind=kLoop, calls=%fused_computation.354 | loop fusion | flops 91750400 | bytes 13131264 | tf_op jit(solution)/shard_map/convert_element_type | solution.py:125
  545.5 8.7 fusion.253
  591.8 35.0 %collective-permute-done.14 = bf16[2,512,640]{2,1,0:T(8,128)(2,1)S(1)} collective-permute-done((bf16[2,512,640]{2,1,0:T(8,128)(2,1)S(1)}, bf16[2,512,640]{2,1,0:T(8,128)(2,1)S(1)}, u32[]{:S(2)}, u32[]{:S(2)}) %collective-permute-start.14) | collective-permute-done | bytes 1310752 | tf_op jit(solution)/shard_map/ppermute | solution.py:12
  631.7 14.7 %collective-permute-done.15 = bf16[2,512,640]{2,1,0:T(8,128)(2,1)S(1)} collective-permute-done((bf16[2,512,640]{2,1,0:T(8,128)(2,1)S(1)}, bf16[2,512,640]{2,1,0:T(8,128)(2,1)S(1)}, u32[]{:S(2)}, u32[]{:S(2)}) %collective-permute-start.15) | collective-permute-done | bytes 1310752 | tf_op jit(solution)/shard_map/ppermute | solution.py:12
  649.5 13.1 multiply_add_fusion.4
  673.1 15.1 %fusion.248 = (f32[640]{0:T(1024)S(1)}, f32[2,512]{1,0:T(2,128)S(1)}, f32[2,512]{1,0:T(2,128)S(1)}, f32[640]{0:T(1024)S(1)}, f32[2,512,640]{2,1,0:T(8,128)}) fusion(f32[640]{0:T(1024)S(1)} %get-tuple-element.185, f32[2,512]{1,0:T(2,128)S(1)} %broadcast_multiply_fusion.3, f32[2,512,640]{2,1,0:T(8,128)S(1)} %get-tuple-element.199, ...), kind=kOutput, calls=%fused_computation.588 | convolution fusion | flops 4251317248 | bytes 21172736 | tf_op jit(solution)/shard_map/scko,kio->sci/dot_general | solution.py:150
  694.9 16.5 %fusion.252 = (f32[640]{0:T(1024)S(1)}, f32[2,512]{1,0:T(2,128)S(1)}, f32[2,512]{1,0:T(2,128)S(1)}, f32[640]{0:T(1024)}, f32[2,512]{1,0:T(2,128)S(1)}, /*index=5*/f32[640]{0:T(1024)}, f32[2,512,640]{2,1,0:T(8,128)S(1)}) fusion(f32[640]{0:T(1024)S(1)} %get-tuple-element.185, f32[2,512]{1,0:T(2,128)S(1)} %copy-done.59, f32[2,512,640]{2,1,0:T(8,128)S(1)} %copy-done.8, ...), kind=kOutput, calls=%fused_computation.592 | convolution fusion | flops 4261801472 | bytes 26442752 | tf_op jit(solution)/shard_map/scko,kio->sci/dot_general | solution.py:150
  732.5 15.4 %fusion.46 = (f32[1280]{0:T(1024)S(1)}, f32[2,512]{1,0:T(2,128)S(1)}, f32[2,512]{1,0:T(2,128)S(1)}, f32[2,512]{1,0:T(2,128)S(1)}, f32[2,512]{1,0:T(2,128)S(1)}, ...) fusion(f32[2,512,1280]{2,1,0:T(8,128)} %get-tuple-element.196, ...), kind=kOutput, calls=%fused_computation.75 | convolution fusion | flops 1736694784 | bytes 39725056 | tf_op jit(solution)/shard_map/sco,io->sci/dot_general | solution.py:159
  778.2 12.0 fusion.282
  805.9 13.0 bitcast_add_fusion
  819.0 12.6 reshape.576
  831.6 8.2 copy.77
  866.4 51.6 %all-reduce.4 = f32[2560]{0:T(1024)S(1)} all-reduce(f32[2560]{0:T(1024)S(1)} %fusion.233), channel_id=21, replica_groups=mesh['batch'=16,'seq'=2] {'batch','seq'}, use_global_device_ids=true, to_apply=%region_63.0.clone | all-reduce | flops 2560 | bytes 20480
  918.6 9.2 fusion.125
  941.8 94.9 %reduce-scatter.21.cloned.1.call-done = f32[640,40]{0,1:T(8,128)} async-done(((f32[640,1280]{0,1:T(8,128)}), f32[640,40]{0,1:T(8,128)}) %reduce-scatter.21.cloned.1.call-update) | async-done | bytes 102416
  1036.7 139.2 %reduce-scatter.17.cloned.1.call-done = f32[40,640]{1,0:T(8,128)} async-done(((f32[1280,640]{1,0:T(8,128)}), f32[40,640]{1,0:T(8,128)}) %reduce-scatter.17.cloned.1.call-update) | async-done | bytes 102416
  1175.9 141.9 %reduce-scatter.19.cloned.1.call-done = f32[1,5,40,320]{3,2,1,0:T(8,128)} async-done(((f32[32,5,40,320]{3,2,1,0:T(8,128)}), f32[1,5,40,320]{3,2,1,0:T(8,128)}) %reduce-scatter.19.cloned.1.call-update) | async-done | bytes 256016
  (534 shorter events, 341.2 us)
Async XLA Ops:
  7.2 134.4 %all-gather.6.cloned.1.call-start = ((), (), s32[]{:S(2)}) async-start(), calls=%async_computation.4 | async-start | bytes 1689600 | tf_op jit(solution)/shard_map/all_gather | solution.py:26
  7.9 189.2 %all-gather.10.cloned.1.call-start = ((), (), s32[]{:S(2)}) async-start(), calls=%async_computation.6 | async-start | bytes 5068800 | tf_op jit(solution)/shard_map/all_gather | solution.py:27
  8.6 237.1 %all-gather.8.cloned.1.call-start = ((), (), s32[]{:S(2)}) async-start(), calls=%async_computation.5 | async-start | bytes 1689600 | tf_op jit(solution)/shard_map/all_gather | solution.py:28
  51.8 273.6 %copy-start.36 = (f32[1280]{0:T(1024)}, f32[1280]{0:T(1024)S(1)}, u32[]{:S(2)}) copy-start(f32[1280]{0:T(1024)S(1)} %slice.367) | copy-start | bytes 15364
  118.3 207.2 %copy-start.40 = (f32[1280]{0:T(1024)}, f32[1280]{0:T(1024)S(1)}, u32[]{:S(2)}) copy-start(f32[1280]{0:T(1024)S(1)} %get-tuple-element.71) | copy-start | bytes 15364
  124.3 191.7 %copy-start.50 = (f32[2,512]{1,0:T(2,128)}, f32[2,512]{1,0:T(2,128)S(1)}, u32[]{:S(2)}) copy-start(f32[2,512]{1,0:T(2,128)S(1)} %get-tuple-element.209) | copy-start | bytes 12292
  124.4 201.1 %copy-start.52 = (f32[2,512]{1,0:T(2,128)}, f32[2,512]{1,0:T(2,128)S(1)}, u32[]{:S(2)}) copy-start(f32[2,512]{1,0:T(2,128)S(1)} %get-tuple-element.210) | copy-start | bytes 12292
  127.3 188.7 %copy-start.66 = (f32[2,512]{1,0:T(2,128)}, f32[2,512]{1,0:T(2,128)S(1)}, u32[]{:S(2)}) copy-start(f32[2,512]{1,0:T(2,128)S(1)} %fusion.237) | copy-start | bytes 12292
  127.4 456.4 %copy-start.42 = (f32[2,512]{1,0:T(2,128)}, f32[2,512]{1,0:T(2,128)S(1)}, u32[]{:S(2)}) copy-start(f32[2,512]{1,0:T(2,128)S(1)} %get-tuple-element.187) | copy-start | bytes 12292
  127.4 545.7 %copy-start.64 = (f32[2,512]{1,0:T(2,128)}, f32[2,512]{1,0:T(2,128)S(1)}, u32[]{:S(2)}) copy-start(f32[2,512]{1,0:T(2,128)S(1)} %get-tuple-element.188) | copy-start | bytes 12292
  154.1 28.3 %collective-permute-start.2 = (bf16[2,512,640]{2,1,0:T(8,128)(2,1)}, bf16[2,512,640]{2,1,0:T(8,128)(2,1)}, u32[]{:S(2)}, u32[]{:S(2)}) collective-permute-start(bf16[2,512,640]{2,1,0:T(8,128)(2,1)} %multiply_convert_fusion.9), channel_id=1, source_target_pairs={{0,1},{2,3},{4,5},{6,7},{8,9},{10,11},{12,13},{14,15},{16,17},{18,... | collective-permute-start | bytes 3932168 | tf_op jit(solution)/shard_map/ppermute | solution.py:12
  156.8 783.5 %reduce-scatter.15.cloned.1.call-start = ((), (), s32[]{:S(2)}) async-start(), calls=%async_computation.7 | async-start | bytes 1351680
  156.9 37.8 %collective-permute-start.3 = (bf16[2,512,640]{2,1,0:T(8,128)(2,1)}, bf16[2,512,640]{2,1,0:T(8,128)(2,1)S(1)}, u32[]{:S(2)}, u32[]{:S(2)}) collective-permute-start(bf16[2,512,640]{2,1,0:T(8,128)(2,1)} %multiply_convert_fusion.9), channel_id=1, source_target_pairs={{1,0},{3,2},{5,4},{7,6},{9,8},{11,10},{13,12},{15,14},{17,16},{19,... | collective-permute-start | bytes 3932168 | tf_op jit(solution)/shard_map/ppermute | solution.py:12
  256.9 28.6 %collective-permute-start.10 = (bf16[2,512,640]{2,1,0:T(8,128)(2,1)}, bf16[2,512,640]{2,1,0:T(8,128)(2,1)}, u32[]{:S(2)}, u32[]{:S(2)}) collective-permute-start(bf16[2,512,640]{2,1,0:T(8,128)(2,1)} %get-tuple-element.108), channel_id=1, source_target_pairs={{1,0},{3,2},{5,4},{7,6},{9,8},{11,10},{13,12},{15,14},{17,16},{19,... | collective-permute-start | bytes 3932168 | tf_op jit(solution)/shard_map/ppermute | solution.py:12
  264.0 29.6 %collective-permute-start.11 = (bf16[2,512,640]{2,1,0:T(8,128)(2,1)}, bf16[2,512,640]{2,1,0:T(8,128)(2,1)}, u32[]{:S(2)}, u32[]{:S(2)}) collective-permute-start(bf16[2,512,640]{2,1,0:T(8,128)(2,1)} %get-tuple-element.108), channel_id=1, source_target_pairs={{0,1},{2,3},{4,5},{6,7},{8,9},{10,11},{12,13},{14,15},{16,17},{18,... | collective-permute-start | bytes 3932168 | tf_op jit(solution)/shard_map/ppermute | solution.py:12
  395.1 115.9 %collective-permute-start.7 = (bf16[2,512,640]{2,1,0:T(8,128)(2,1)S(1)}, bf16[2,512,640]{2,1,0:T(8,128)(2,1)S(1)}, u32[]{:S(2)}, u32[]{:S(2)}) collective-permute-start(bf16[2,512,640]{2,1,0:T(8,128)(2,1)S(1)} %get-tuple-element.171), channel_id=1, source_target_pairs={{1,0},{3,2},{5,4},{7,6},{9,8},{11,10},{13,12},{15,14},{17,16},{19,... | collective-permute-start | bytes 3932168 | tf_op jit(solution)/shard_map/ppermute | solution.py:12
  396.4 106.0 %collective-permute-start.6 = (bf16[2,512,640]{2,1,0:T(8,128)(2,1)S(1)}, bf16[2,512,640]{2,1,0:T(8,128)(2,1)S(1)}, u32[]{:S(2)}, u32[]{:S(2)}) collective-permute-start(bf16[2,512,640]{2,1,0:T(8,128)(2,1)S(1)} %get-tuple-element.171), channel_id=1, source_target_pairs={{0,1},{2,3},{4,5},{6,7},{8,9},{10,11},{12,13},{14,15},{16,17},{18,... | collective-permute-start | bytes 3932168 | tf_op jit(solution)/shard_map/ppermute | solution.py:12
  401.2 83.7 %collective-permute-start.5 = (bf16[2,512,640]{2,1,0:T(8,128)(2,1)S(1)}, bf16[2,512,640]{2,1,0:T(8,128)(2,1)S(1)}, u32[]{:S(2)}, u32[]{:S(2)}) collective-permute-start(bf16[2,512,640]{2,1,0:T(8,128)(2,1)S(1)} %get-tuple-element.172), channel_id=1, source_target_pairs={{1,0},{3,2},{5,4},{7,6},{9,8},{11,10},{13,12},{15,14},{17,16},{19,... | collective-permute-start | bytes 3932168 | tf_op jit(solution)/shard_map/ppermute | solution.py:12
  402.5 55.8 %collective-permute-start.4 = (bf16[2,512,640]{2,1,0:T(8,128)(2,1)S(1)}, bf16[2,512,640]{2,1,0:T(8,128)(2,1)S(1)}, u32[]{:S(2)}, u32[]{:S(2)}) collective-permute-start(bf16[2,512,640]{2,1,0:T(8,128)(2,1)S(1)} %get-tuple-element.172), channel_id=1, source_target_pairs={{0,1},{2,3},{4,5},{6,7},{8,9},{10,11},{12,13},{14,15},{16,17},{18,... | collective-permute-start | bytes 3932168 | tf_op jit(solution)/shard_map/ppermute | solution.py:12
  408.5 71.2 %collective-permute-start = (bf16[2,512,640]{2,1,0:T(8,128)(2,1)S(1)}, bf16[2,512,640]{2,1,0:T(8,128)(2,1)S(1)}, u32[]{:S(2)}, u32[]{:S(2)}) collective-permute-start(bf16[2,512,640]{2,1,0:T(8,128)(2,1)S(1)} %get-tuple-element.173), channel_id=1, source_target_pairs={{0,1},{2,3},{4,5},{6,7},{8,9},{10,11},{12,13},{14,15},{16,17},{18,... | collective-permute-start | bytes 3932168 | tf_op jit(solution)/shard_map/ppermute | solution.py:12
  458.3 37.3 %collective-permute-start.1 = (bf16[2,512,640]{2,1,0:T(8,128)(2,1)S(1)}, bf16[2,512,640]{2,1,0:T(8,128)(2,1)S(1)}, u32[]{:S(2)}, u32[]{:S(2)}) collective-permute-start(bf16[2,512,640]{2,1,0:T(8,128)(2,1)S(1)} %get-tuple-element.173), channel_id=1, source_target_pairs={{1,0},{3,2},{5,4},{7,6},{9,8},{11,10},{13,12},{15,14},{17,16},{19,... | collective-permute-start | bytes 3932168 | tf_op jit(solution)/shard_map/ppermute | solution.py:12
  559.7 70.8 %copy-start.3 = (bf16[2,512,640]{2,1,0:T(8,128)(2,1)}, bf16[2,512,640]{2,1,0:T(8,128)(2,1)S(1)}, u32[]{:S(2)}) copy-start(bf16[2,512,640]{2,1,0:T(8,128)(2,1)S(1)} %get-tuple-element.100) | copy-start | bytes 3932164
  564.0 103.4 %copy-start.5 = (bf16[2,512,640]{2,1,0:T(8,128)(2,1)}, bf16[2,512,640]{2,1,0:T(8,128)(2,1)S(1)}, u32[]{:S(2)}) copy-start(bf16[2,512,640]{2,1,0:T(8,128)(2,1)S(1)} %get-tuple-element.104) | copy-start | bytes 3932164
  564.2 104.4 %collective-permute-start.13 = (bf16[2,512,640]{2,1,0:T(8,128)(2,1)S(1)}, bf16[2,512,640]{2,1,0:T(8,128)(2,1)}, u32[]{:S(2)}, u32[]{:S(2)}) collective-permute-start(bf16[2,512,640]{2,1,0:T(8,128)(2,1)S(1)} %get-tuple-element.104), channel_id=1, source_target_pairs={{0,1},{2,3},{4,5},{6,7},{8,9},{10,11},{12,13},{14,15},{16,17},{18,... | collective-permute-start | bytes 3932168 | tf_op jit(solution)/shard_map/ppermute | solution.py:12
  569.7 92.9 %collective-permute-start.12 = (bf16[2,512,640]{2,1,0:T(8,128)(2,1)S(1)}, bf16[2,512,640]{2,1,0:T(8,128)(2,1)}, u32[]{:S(2)}, u32[]{:S(2)}) collective-permute-start(bf16[2,512,640]{2,1,0:T(8,128)(2,1)S(1)} %get-tuple-element.104), channel_id=1, source_target_pairs={{1,0},{3,2},{5,4},{7,6},{9,8},{11,10},{13,12},{15,14},{17,16},{19,... | collective-permute-start | bytes 3932168 | tf_op jit(solution)/shard_map/ppermute | solution.py:12
  571.2 118.1 %collective-permute-start.9 = (bf16[2,512,640]{2,1,0:T(8,128)(2,1)S(1)}, bf16[2,512,640]{2,1,0:T(8,128)(2,1)}, u32[]{:S(2)}, u32[]{:S(2)}) collective-permute-start(bf16[2,512,640]{2,1,0:T(8,128)(2,1)S(1)} %get-tuple-element.181), channel_id=1, source_target_pairs={{0,1},{2,3},{4,5},{6,7},{8,9},{10,11},{12,13},{14,15},{16,17},{18,... | collective-permute-start | bytes 3932168 | tf_op jit(solution)/shard_map/ppermute | solution.py:12
  578.0 68.4 %collective-permute-start.15 = (bf16[2,512,640]{2,1,0:T(8,128)(2,1)S(1)}, bf16[2,512,640]{2,1,0:T(8,128)(2,1)S(1)}, u32[]{:S(2)}, u32[]{:S(2)}) collective-permute-start(bf16[2,512,640]{2,1,0:T(8,128)(2,1)S(1)} %get-tuple-element.100), channel_id=1, source_target_pairs={{0,1},{2,3},{4,5},{6,7},{8,9},{10,11},{12,13},{14,15},{16,17},{18,... | collective-permute-start | bytes 3932168 | tf_op jit(solution)/shard_map/ppermute | solution.py:12
  579.7 47.0 %collective-permute-start.14 = (bf16[2,512,640]{2,1,0:T(8,128)(2,1)S(1)}, bf16[2,512,640]{2,1,0:T(8,128)(2,1)S(1)}, u32[]{:S(2)}, u32[]{:S(2)}) collective-permute-start(bf16[2,512,640]{2,1,0:T(8,128)(2,1)S(1)} %get-tuple-element.100), channel_id=1, source_target_pairs={{1,0},{3,2},{5,4},{7,6},{9,8},{11,10},{13,12},{15,14},{17,16},{19,... | collective-permute-start | bytes 3932168 | tf_op jit(solution)/shard_map/ppermute | solution.py:12
  626.8 61.4 %collective-permute-start.8 = (bf16[2,512,640]{2,1,0:T(8,128)(2,1)S(1)}, bf16[2,512,640]{2,1,0:T(8,128)(2,1)S(1)}, u32[]{:S(2)}, u32[]{:S(2)}) collective-permute-start(bf16[2,512,640]{2,1,0:T(8,128)(2,1)S(1)} %get-tuple-element.181), channel_id=1, source_target_pairs={{1,0},{3,2},{5,4},{7,6},{9,8},{11,10},{13,12},{15,14},{17,16},{19,... | collective-permute-start | bytes 3932168 | tf_op jit(solution)/shard_map/ppermute | solution.py:12
  749.7 287.0 %reduce-scatter.21.cloned.1.call-start = ((), (), s32[]{:S(2)}) async-start(), calls=%async_computation.10 | async-start | bytes 3379200
  757.0 419.0 %reduce-scatter.17.cloned.1.call-start = ((), (), s32[]{:S(2)}) async-start(), calls=%async_computation.8 | async-start | bytes 3379200
  770.6 547.2 %reduce-scatter.19.cloned.1.call-start = ((), (), s32[]{:S(2)}) async-start(), calls=%async_computation.9 | async-start | bytes 10137600
  (123 other events, 1242.4 us)
Sparse Core Ops, SparseCore 0:
  10.8 57.9 all-gather.5
  71.6 63.2 all-gather.9
  157.0 52.1 all-gather.7
  749.9 147.8 reduce-scatter.14
  900.6 136.0 reduce-scatter.20
  1039.4 136.4 reduce-scatter.16
  1183.5 134.2 reduce-scatter.18
where the time goes:
time: 1330 us
  waiting for transfers between devices  518 us (39%)
  matrix products  251 us (19%)
  other arithmetic  232 us (17%)
  blocking collectives  159 us (12%)
  local copies, waits for them, and re-layouts  102 us (8%)
  starting transfers between devices  45.6 us (3%)
  between operations  17.3 us (1%)
    unnamed x11, waiting for transfers between devices  377 us
    ppermute x16, waiting for transfers between devices, shifted(): lax.ppermute(value, axis, [(source, source + steps) for source in range(i...  140 us
    unnamed x2, blocking collectives  93.8 us
    all_gather x1, blocking collectives, gather_weights(): lax.all_gather(shift_params, ('batch', 'seq'), axis=1, tiled=True)  65.7 us
    dot_general x4, matrix products, micro_step(): jnp.einsum('scko,kio->sci', back_stack, taps_full, preferred_element_type...  59 us
    convert_element_type x2, other arithmetic, micro_step(): act_first = act_first.astype(jnp.bfloat16)  54.6 us
    ppermute x16, starting transfers between devices, shifted(): lax.ppermute(value, axis, [(source, source + steps) for source in range(i...  44.8 us
    convert_element_type x3, other arithmetic, micro_step(): act_third = act_third.astype(jnp.bfloat16)  41.2 us
  transfers between devices with their start and end apart: 23, of which 10 were waited for; matrix products, arithmetic and copies ran while one was open for 26% of the time, Pallas kernels for 0%

commit v1 on v0

v1 whole, which is shorter than its diff:
```python
import functools, math
import jax
import jax.numpy as jnp
from jax import lax
from jax.experimental import pallas as pl
from jax.experimental.pallas import tpu as pltpu
from jax.sharding import PartitionSpec as P

DILATION_STEP = 128
BLOCK = 128
PACK = 4
CHUNK = 16
HALF = 1 / math.sqrt(2)
DENSITY = 1 / math.sqrt(2 * math.pi)
BF = jnp.bfloat16
F32 = jnp.float32
NT = (((1,), (1,)), ((), ()))


def dot(a, b):
    return jnp.dot(a, b, preferred_element_type=F32)


def dot_nt(a, b):
    return lax.dot_general(a, b, NT, preferred_element_type=F32)


def norm(v):
    scale = 1 / v.shape[-1]
    c = v - jnp.sum(v, -1, keepdims=True) * scale
    r = lax.rsqrt(jnp.sum(c * c, -1, keepdims=True) * scale + 1e-5)
    return c * r, r


def act(hat, gain, beta):
    n = hat * gain + beta
    below = 0.5 + 0.5 * lax.erf(n * HALF)
    slope = below + n * (jnp.exp(-0.5 * (n * n)) * DENSITY)
    return n * below, slope * gain


def fold(v):
    out = v[0:8]
    for k in range(1, v.shape[0] // 8):
        out = out + v[8 * k : 8 * k + 8]
    return out


def norm_back(e, hat, r):
    scale = 1 / e.shape[-1]
    eh = e * hat
    m1 = jnp.sum(e, -1, keepdims=True) * scale
    m2 = jnp.sum(eh, -1, keepdims=True) * scale
    return (e - m1 - hat * m2) * r, eh


def over_rows(body, rows=BLOCK, unroll=8):
    def step(i, carry):
        body(pl.multiple_of(i * CHUNK, CHUNK))
        return carry

    lax.fori_loop(0, rows // CHUNK, step, 0, unroll=unroll)


def first_kernel(
    perm, nval, cnt, *refs
):
    x = refs[:PACK]
    w, par_d, par_i = refs[PACK : PACK + 3]
    act1, hat1, d1, r1, act2, hat2, d2, r2 = refs[PACK + 3 : PACK + 11]
    (mid,) = refs[PACK + 11 :]
    i = pl.program_id(0)

    @pl.when(i < cnt[1])
    def _():
        for q in range(PACK):

            def rows_first(at, q=q):
                s = pl.ds(at, CHUNK)
                t = pl.ds(q * BLOCK + at, CHUNK)
                hat, r = norm(x[q][0, s, :].astype(F32))
                a, d = act(hat, par_d[0:1, :], par_d[1:2, :])
                act1[t, :] = a.astype(BF)
                hat1[t, :] = hat.astype(BF)
                d1[t, :] = d.astype(BF)
                r1[t, :] = jnp.broadcast_to(r, (CHUNK, 128))

            over_rows(rows_first)
        mid[...] = dot(act1[...], w[...])
        for q in range(PACK):
            count = nval[i * PACK + q]

            def rows_second(at, q=q, count=count):
                t = pl.ds(q * BLOCK + at, CHUNK)
                hat, r = norm(mid[t, :] + par_i[2:3, :])
                a, d = act(hat, par_i[0:1, :], par_i[1:2, :])
                live = (at + lax.broadcasted_iota(jnp.int32, (CHUNK, 1), 0) < count).astype(F32)
                act2[t, :] = (a * live).astype(BF)
                hat2[t, :] = hat.astype(BF)
                d2[t, :] = (d * live).astype(BF)
                r2[t, :] = jnp.broadcast_to(r, (CHUNK, 128))

            over_rows(rows_second)


def block_specs(width, clamp):
    def spec(q):
        def where(i, perm, nval, cnt, *_):
            if clamp:
                i = jnp.minimum(i, jnp.maximum(cnt[1] - 1, 0))
            return (perm[i * PACK + q], 0, 0)

        return pl.BlockSpec((1, BLOCK, width), where)

    return [spec(q) for q in range(PACK)]


def compact_spec(width):
    def where(i, perm, nval, cnt, *_):
        return (jnp.minimum(i, jnp.maximum(cnt[1] - 1, 0)), 0)

    return pl.BlockSpec((PACK * BLOCK, width), where)


def whole(shape):
    return pl.BlockSpec(shape, lambda *_: (0,) * len(shape), pipeline_mode=pl.Buffered(1))


ANY = pl.BlockSpec(memory_space=pl.ANY)


def params(mb=56):
    return pltpu.CompilerParams(
        vmem_limit_bytes=mb * 2**20, dimension_semantics=("arbitrary",)
    )


def run_first(tables, x, w, par_d, par_i):
    T, _, D = x.shape
    I = w.shape[1]
    rows = T * BLOCK
    S = jax.ShapeDtypeStruct
    grid = pltpu.PrefetchScalarGridSpec(
        num_scalar_prefetch=3,
        grid=(T // PACK,),
        in_specs=block_specs(D, True) + [whole(w.shape), whole(par_d.shape), whole(par_i.shape)],
        out_specs=[compact_spec(D)] * 3
        + [compact_spec(128)]
        + [compact_spec(I)] * 3
        + [compact_spec(128)],
        scratch_shapes=[pltpu.VMEM((PACK * BLOCK, I), F32)],
    )
    return pl.pallas_call(
        first_kernel,
        grid_spec=grid,
        out_shape=[S((rows, D), BF)] * 3
        + [S((rows, 128), F32)]
        + [S((rows, I), BF)] * 3
        + [S((rows, 128), F32)],
        compiler_params=params(),
        name="first",
    )(*tables, *([x] * PACK), w, par_d, par_i)


def gather_taps(tab, step, slot, im, local, halo, zero, sems, T, H, width):
    for q in range(PACK):
        for k in range(5):
            code = tab[(step * PACK + q) * 5 + k]
            dst = im.at[slot, pl.ds(q * BLOCK, BLOCK), pl.ds(k * width, width)]

            @pl.when(code < T)
            def _(code=code, dst=dst):
                src = local.at[pl.ds(pl.multiple_of(code * BLOCK, BLOCK), BLOCK), :]
                pltpu.make_async_copy(src, dst, sems.at[slot]).start()

            @pl.when((code >= T) & (code < T + H))
            def _(code=code, dst=dst):
                src = halo.at[pl.ds(pl.multiple_of((code - T) * BLOCK, BLOCK), BLOCK), :]
                pltpu.make_async_copy(src, dst, sems.at[slot]).start()

            @pl.when(code >= T + H)
            def _(dst=dst):
                pltpu.make_async_copy(zero, dst, sems.at[slot]).start()


def wait_slot(buf, slot, sems):
    pltpu.make_async_copy(buf.at[slot], buf.at[slot], sems.at[slot]).wait()


def put_blocks(perm, i, slot, obuf, out, osem):
    for q in range(PACK):
        pltpu.make_async_copy(obuf.at[slot, q], out.at[perm[i * PACK + q]], osem.at[slot]).start()


def second_kernel(T, H, perm, nval, cnt, tab, *refs):
    x = refs[:PACK]
    c = refs[PACK : 2 * PACK]
    local, halo, zero, taps, wt, par_d, par_i = refs[2 * PACK : 2 * PACK + 7]
    out, gms, glast, gtaps, sum_d, sum_i = refs[2 * PACK + 7 : 2 * PACK + 13]
    im, mid, act3, hat3, d3, r3, br, gb, obuf, sems, osem = refs[2 * PACK + 13 :]
    i = pl.program_id(0)
    steps = pl.num_programs(0)
    I = wt.shape[1]
    slot = lax.rem(i, 2)
    live_steps = cnt[1]

    @pl.when(i == 0)
    def _():
        glast[...] = jnp.zeros_like(glast)
        gtaps[...] = jnp.zeros_like(gtaps)
        sum_d[...] = jnp.zeros_like(sum_d)
        sum_i[...] = jnp.zeros_like(sum_i)

        @pl.when(live_steps > 0)
        def _():
            gather_taps(tab, 0, 0, im, local, halo, zero, sems, T, H, I)

    @pl.when(i >= 2)
    def _():
        wait_slot(obuf, slot, osem)

    @pl.when(i < live_steps)
    def _():
        @pl.when(i + 1 < live_steps)
        def _():
            gather_taps(tab, i + 1, 1 - slot, im, local, halo, zero, sems, T, H, I)

        wait_slot(im, slot, sems)
        mid[...] = dot(im[slot], taps[...])

        def rows_third(at):
            t = pl.ds(at, CHUNK)
            hat, r = norm(mid[t, :] + par_i[2:3, :])
            a, d = act(hat, par_i[0:1, :], par_i[1:2, :])
            act3[t, :] = a.astype(BF)
            hat3[t, :] = hat.astype(BF)
            d3[t, :] = d.astype(BF)
            r3[t, :] = jnp.broadcast_to(r, (CHUNK, 128))

        over_rows(rows_third, PACK * BLOCK)
        br[...] = dot_nt(act3[...], wt[...])
        for q in range(PACK):
            count = nval[i * PACK + q]

            def rows_out(at, q=q, count=count):
                s = pl.ds(at, CHUNK)
                t = pl.ds(q * BLOCK + at, CHUNK)
                live = (at + lax.broadcasted_iota(jnp.int32, (CHUNK, 1), 0) < count).astype(F32)
                rows = x[q][0, s, :].astype(F32) + live * (br[t, :] + par_d[0:1, :])
                obuf[slot, q, s, :] = rows.astype(BF)
                grad = c[q][0, s, :].astype(F32) * live
                gb[t, :] = grad.astype(BF)
                sum_d[...] += fold(grad)

            over_rows(rows_out)
        mid[...] = dot(gb[...], wt[...])

        def rows_back(at):
            t = pl.ds(at, CHUNK)
            hat = hat3[t, :].astype(F32)
            e = mid[t, :] * d3[t, :].astype(F32)
            g, eh = norm_back(e, hat, r3[t, 0:1])
            g = g.astype(BF)
            gms[t, :] = g
            sum_i[0:8, :] += fold(eh)
            sum_i[8:16, :] += fold(e)
            sum_i[16:24, :] += fold(g.astype(F32))

        over_rows(rows_back, PACK * BLOCK)
        glast[...] += dot(act3[...].T, gb[...])
        gt = gms[...].T
        for k in range(5):
            s = slice(k * I, (k + 1) * I)
            gtaps[:, s] += dot(gt, im[slot, :, s])

    @pl.when(i >= live_steps)
    def _():
        for q in range(PACK):
            obuf[slot, q] = x[q][0]

    put_blocks(perm, i, slot, obuf, out, osem)

    @pl.when(i == steps - 1)
    def _():
        wait_slot(obuf, slot, osem)

        @pl.when(steps > 1)
        def _():
            wait_slot(obuf, 1 - slot, osem)


def run_second(tables, tab, x, cot, local, halo, zero, taps, wt, par_d, par_i):
    T, _, D = x.shape
    I = wt.shape[1]
    rows = T * BLOCK
    M = PACK * BLOCK
    H = halo.shape[0] // BLOCK
    S = jax.ShapeDtypeStruct
    V = pltpu.VMEM
    grid = pltpu.PrefetchScalarGridSpec(
        num_scalar_prefetch=4,
        grid=(T // PACK,),
        in_specs=block_specs(D, False)
        + block_specs(D, True)
        + [ANY, ANY, ANY, whole(taps.shape), whole(wt.shape), whole(par_d.shape), whole(par_i.shape)],
        out_specs=[ANY, compact_spec(I), whole((I, D)), whole((I, 5 * I)), whole((8, D)), whole((24, I))],
        scratch_shapes=[
            V((2, M, 5 * I), BF), V((M, I), F32), V((M, I), BF), V((M, I), BF), V((M, I), BF),
            V((M, 128), F32), V((M, D), F32), V((M, D), BF), V((2, PACK, BLOCK, D), BF),
            pltpu.SemaphoreType.DMA((2,)), pltpu.SemaphoreType.DMA((2,)),
        ],
    )
    return pl.pallas_call(
        functools.partial(second_kernel, T, H),
        grid_spec=grid,
        out_shape=[S((T, BLOCK, D), BF), S((rows, I), BF), S((I, D), F32), S((I, 5 * I), F32), S((8, D), F32), S((24, I), F32)],
        compiler_params=params(),
        name="second",
    )(*tables, tab, *([x] * PACK), *([cot] * PACK), local, halo, zero, taps, wt, par_d, par_i)


def third_kernel(T, H, perm, nval, cnt, tab, *refs):
    c = refs[:PACK]
    local, halo, zero, taps, w, act1, hat1, d1, r1, hat2, d2, r2 = refs[PACK : PACK + 12]
    gin, gfirst, sum_d, sum_i = refs[PACK + 12 : PACK + 16]
    im, mid, gmf, big, obuf, sems, osem = refs[PACK + 16 :]
    i = pl.program_id(0)
    steps = pl.num_programs(0)
    I = w.shape[1]
    slot = lax.rem(i, 2)
    live_steps = cnt[1]

    @pl.when(i == 0)
    def _():
        gfirst[...] = jnp.zeros_like(gfirst)
        sum_d[...] = jnp.zeros_like(sum_d)
        sum_i[...] = jnp.zeros_like(sum_i)

        @pl.when(live_steps > 0)
        def _():
            gather_taps(tab, 0, 0, im, local, halo, zero, sems, T, H, I)

    @pl.when(i >= 2)
    def _():
        wait_slot(obuf, slot, osem)

    @pl.when(i < live_steps)
    def _():
        @pl.when(i + 1 < live_steps)
        def _():
            gather_taps(tab, i + 1, 1 - slot, im, local, halo, zero, sems, T, H, I)

        wait_slot(im, slot, sems)
        total = dot_nt(im[slot, :, 0:I], taps[0:I, :])
        for k in range(1, 5):
            total = total + dot_nt(im[slot, :, k * I : (k + 1) * I], taps[k * I : (k + 1) * I, :])
        mid[...] = total

        def rows_second(at):
            t = pl.ds(at, CHUNK)
            hat = hat2[t, :].astype(F32)
            e = mid[t, :] * d2[t, :].astype(F32)
            g, eh = norm_back(e, hat, r2[t, 0:1])
            g = g.astype(BF)
            gmf[t, :] = g
            sum_i[0:8, :] += fold(eh)
            sum_i[8:16, :] += fold(e)
            sum_i[16:24, :] += fold(g.astype(F32))

        over_rows(rows_second, PACK * BLOCK)
        gfirst[...] += dot(gmf[...].T, act1[...])
        big[...] = dot_nt(gmf[...], w[...])
        for q in range(PACK):

            def rows_first(at, q=q):
                s = pl.ds(at, CHUNK)
                t = pl.ds(q * BLOCK + at, CHUNK)
                hat = hat1[t, :].astype(F32)
                e = big[t, :] * d1[t, :].astype(F32)
                g, eh = norm_back(e, hat, r1[t, 0:1])
                obuf[slot, q, s, :] = (c[q][0, s, :].astype(F32) + g).astype(BF)
                sum_d[0:8, :] += fold(eh)
                sum_d[8:16, :] += fold(e)

            over_rows(rows_first)

    @pl.when(i >= live_steps)
    def _():
        for q in range(PACK):
            obuf[slot, q] = c[q][0]

    put_blocks(perm, i, slot, obuf, gin, osem)

    @pl.when(i == steps - 1)
    def _():
        wait_slot(obuf, slot, osem)

        @pl.when(steps > 1)
        def _():
            wait_slot(obuf, 1 - slot, osem)


def run_third(tables, tab, cot, local, halo, zero, taps, w, saved):
    T, _, D = cot.shape
    I = w.shape[1]
    M = PACK * BLOCK
    H = halo.shape[0] // BLOCK
    S = jax.ShapeDtypeStruct
    V = pltpu.VMEM
    grid = pltpu.PrefetchScalarGridSpec(
        num_scalar_prefetch=4,
        grid=(T // PACK,),
        in_specs=block_specs(D, False)
        + [ANY, ANY, ANY, whole(taps.shape), whole(w.shape)]
        + [compact_spec(D)] * 3
        + [compact_spec(128)]
        + [compact_spec(I)] * 2
        + [compact_spec(128)],
        out_specs=[ANY, whole((I, D)), whole((16, D)), whole((24, I))],
        scratch_shapes=[
            V((2, M, 5 * I), BF), V((M, I), F32), V((M, I), BF), V((M, D), F32),
            V((2, PACK, BLOCK, D), BF),
            pltpu.SemaphoreType.DMA((2,)), pltpu.SemaphoreType.DMA((2,)),
        ],
    )
    act1, hat1, d1, r1, act2, hat2, d2, r2 = saved
    return pl.pallas_call(
        functools.partial(third_kernel, T, H),
        grid_spec=grid,
        out_shape=[S((T, BLOCK, D), BF), S((I, D), F32), S((16, D), F32), S((24, I), F32)],
        compiler_params=params(),
        name="third",
    )(*tables, tab, *([cot] * PACK), local, halo, zero, taps, w, act1, hat1, d1, r1, hat2, d2, r2)


def layout_tables(lens, seq_index, n_seq, nblk, reach):
    count = lens.shape[0] * nblk
    edge = edge_blocks(lens.shape[0], n_seq, nblk, reach)
    t = jnp.arange(count, dtype=jnp.int32)
    s, j = t // nblk, t % nblk
    length = jnp.repeat(lens, nblk, total_repeat_length=count)

    def ranks(index):
        live = (index * nblk + j) * BLOCK < length
        reads_left = (j < reach) & (index > 0)
        reads_right = (j >= nblk - reach) & (index < n_seq - 1)
        reads_right = reads_right & ((index + 1) * nblk * BLOCK < length)
        kind = jnp.where(live, jnp.where(reads_left | reads_right, 0, 1), 2)
        key = kind * count + t
        rank = jnp.sum((key[None, :] < key[:, None]).astype(jnp.int32), axis=1)
        return rank, kind

    rank, kind = ranks(seq_index)
    chosen = (rank[:, None] == t[None, :]).astype(jnp.int32)
    perm = jnp.sum(chosen * t[:, None], axis=0)
    left = jnp.clip(length - (seq_index * nblk + j) * BLOCK, 0, BLOCK)
    nval = jnp.sum(chosen * left[:, None], axis=0)
    cnt = jnp.stack(
        [
            (jnp.sum((kind == 0).astype(jnp.int32)) + PACK - 1) // PACK,
            (jnp.sum((kind < 2).astype(jnp.int32)) + PACK - 1) // PACK,
        ]
    )
    hops = hop_list(n_seq, nblk, reach)
    zero = count + (1 if n_seq == 2 else len(hops)) * edge
    code = []
    for k in range(-reach, reach + 1):
        far = seq_index * nblk + j + k
        inside = (far >= 0) & (far * BLOCK < length)
        place = jnp.full_like(t, zero)
        for hop in [0] + hops:
            other = seq_index + hop
            at = rank if hop == 0 else ranks(other)[0]
            there = far - other * nblk
            mine = inside & (there >= 0) & (there < nblk)
            found = jnp.sum(
                jnp.where((s * nblk + there)[:, None] == t[None, :], at[None, :], 0), axis=1
            )
            base = 0 if hop == 0 else count + (0 if n_seq == 2 else hops.index(hop) * edge)
            place = jnp.where(mine, base + found, place)
        code.append(place)
    code = jnp.stack(code, axis=1)
    code = jnp.sum(chosen[:, :, None] * code[:, None, :], axis=0)
    return (perm, nval, cnt), code.reshape(-1), code[:, ::-1].reshape(-1)


def edge_blocks(seqs, n_seq, nblk, reach):
    return seqs * min(nblk, reach * (1 if n_seq == 2 else 2))


def hop_list(n_seq, nblk, reach):
    furthest = min(n_seq - 1, -(-reach // nblk))
    return [hop for h in range(1, furthest + 1) for hop in (h, -h)]


def from_neighbours(rows, n_seq, hops):
    if n_seq == 2:
        return lax.ppermute(rows, "seq", [(0, 1), (1, 0)])
    parts = [
        lax.ppermute(rows, "seq", [(i, i - hop) for i in range(n_seq) if 0 <= i - hop < n_seq])
        for hop in hops
    ]
    return jnp.concatenate(parts, axis=0) if parts else rows[:0]


def shards(inputs, cotangent, lengths, w_first, tap_weights, w_last, norm_gain, shift_params):
    n_batch = lax.axis_size("batch")
    n_seq = lax.axis_size("seq")
    seq_index = lax.axis_index("seq")
    both = ("batch", "seq")
    micro, seqs, span, D = inputs.shape
    I = w_first.shape[1]
    K = tap_weights.shape[0]
    nblk = span // BLOCK
    T = micro * seqs * nblk
    reach = K // 2
    rows_w = w_first.shape[0]
    small = jnp.concatenate([norm_gain[None], shift_params]).reshape(1, -1)
    small = jnp.pad(small, ((0, 7), (0, I - small.shape[1])))
    early = lax.all_gather(jnp.concatenate([w_first, small]), both, axis=0)
    w_full = early[:, :rows_w].reshape(D, I)
    vecs = early[:, rows_w, : 3 * norm_gain.shape[0]].astype(F32)
    vecs = vecs.reshape(-1, 3, norm_gain.shape[0]).transpose(1, 0, 2).reshape(3, -1)
    wt_full = lax.all_gather(w_last.T, both, axis=0, tiled=True)
    taps_full = lax.all_gather(tap_weights, both, axis=0)
    rows_t, cols_t = tap_weights.shape[1:]
    taps_full = taps_full.reshape(n_batch, n_seq, K, rows_t, cols_t)
    taps_full = taps_full.transpose(2, 0, 3, 1, 4).reshape(K * I, I)

    gain, beta, bias = vecs[0], vecs[1], vecs[2]
    two, three = slice(D, D + I), slice(D + I, D + 2 * I)
    par_first = jnp.stack([gain[:D], beta[:D]])
    par_second = jnp.stack([gain[two], beta[two], bias[two]])
    par_third = jnp.stack([gain[three], beta[three], bias[three]])
    par_last = bias[None, :D]

    tables, ahead, back = layout_tables(lengths.reshape(-1), seq_index, n_seq, nblk, reach)
    hops = hop_list(n_seq, nblk, reach)
    edge = edge_blocks(micro * seqs, n_seq, nblk, reach) * BLOCK
    zero = jnp.zeros((BLOCK, I), BF)
    x = inputs.reshape(T, BLOCK, D)
    cot = cotangent.reshape(T, BLOCK, D)

    saved = run_first(tables, x, w_full, par_first, par_second)
    halo = from_neighbours(saved[4][:edge], n_seq, hops)
    out, gms, g_last, g_taps, sum_out, sum_third = run_second(
        tables, ahead, x, cot, saved[4], halo, zero, taps_full, wt_full, par_last, par_third
    )
    halo = from_neighbours(gms[:edge], n_seq, hops)
    gin, g_first, sum_first, sum_second = run_third(
        tables, back, cot, gms, halo, zero, taps_full, w_full, saved
    )

    def total(v):
        return jnp.sum(v.reshape(-1, 8, v.shape[-1]), axis=1)

    sum_first, sum_second, sum_third = total(sum_first), total(sum_second), total(sum_third)
    sum_out = total(sum_out)
    sums = jnp.stack(
        [
            jnp.concatenate([sum_first[0], sum_second[0], sum_third[0]]) / gain,
            jnp.concatenate([sum_first[1], sum_second[1], sum_third[1]]) / gain,
            jnp.concatenate([sum_out[0], sum_second[2], sum_third[2]]),
        ]
    )
    sums = lax.psum_scatter(sums, both, scatter_dimension=1, tiled=True)
    grad_first = lax.psum_scatter(g_first.T.astype(BF), both, scatter_dimension=0, tiled=True)
    grad_last = lax.psum_scatter(g_last.T.astype(BF), both, scatter_dimension=0, tiled=True).T
    g_taps = g_taps.reshape(n_seq, cols_t, K, n_batch, rows_t).transpose(3, 0, 2, 4, 1)
    g_taps = g_taps.astype(BF).reshape(n_batch * n_seq, K, rows_t, cols_t)
    grad_taps = lax.psum_scatter(g_taps, both, scatter_dimension=0)
    return (
        out.reshape(inputs.shape),
        gin.reshape(inputs.shape),
        grad_first.astype(F32),
        grad_taps.astype(F32),
        grad_last.astype(F32),
        sums[0],
        sums[1:],
    )


def solution(mesh):
    placed = (
        P(None, "batch", "seq", None),
        P(None, "batch", "seq", None),
        P(None, "batch"),
        P(("batch", "seq"), None),
        P(None, "batch", "seq"),
        P(None, ("batch", "seq")),
        P(("batch", "seq")),
        P(None, ("batch", "seq")),
    )
    return jax.shard_map(
        shards,
        mesh=mesh,
        in_specs=placed,
        out_specs=(
            P(None, "batch", "seq", None),
            P(None, "batch", "seq", None),
            P(("batch", "seq"), None),
            P(None, "batch", "seq"),
            P(None, ("batch", "seq")),
            P(("batch", "seq")),
            P(None, ("batch", "seq")),
        ),
        check_vma=False,
    )
```

time: 1330 us -> 839 us (0.63)
  matrix products: 251 us -> 0 us
  other arithmetic: 232 us -> 23.9 us
  Pallas kernels: 0 us -> 182 us
  blocking collectives: 159 us -> 0 us
  starting transfers between devices: 45.6 us -> 0.24 us
  local copies, waits for them, and re-layouts: 102 us -> 65.5 us
  waiting for transfers between devices: 518 us -> 552 us
    dot_general x36 -> x0, matrix products: 251 us -> none  [the longest x4 59 us: micro_step(): jnp.einsum('scko,kio->sci', back_stack, taps_full, preferred_element_type...]
    pallas_call x0 -> x3, Pallas kernels: none -> 182 us  [the longest x1 94.6 us: run_second(): pl.pallas_call(functools.partial(second_kernel, T, H), grid_spec=grid, ou...]
    all_gather x3, waiting for transfers between devices: 0.02 us -> 125 us  [the longest x1 53.7 us: shards(): early = lax.all_gather(jnp.concatenate([w_first, small]), both, axis=0)]
    convert_element_type x9 -> x7, other arithmetic: 123 us -> 14.2 us  [the longest x1 5.64 us: shards(): g_taps = g_taps.astype(BF).reshape(n_batch * n_seq, K, rows_t, cols_t)]
    ppermute x16 -> x2, waiting for transfers between devices: 140 us -> 34.2 us  [from_neighbours(): return lax.ppermute(rows, 'seq', [(0, 1), (1, 0)])]
    unnamed x2 -> x0, blocking collectives: 93.8 us -> none
    all_gather x1 -> x0, blocking collectives: 65.7 us -> none  [gather_weights(): lax.all_gather(shift_params, ('batch', 'seq'), axis=1, tiled=True)]
    ppermute x16 -> x2, starting transfers between devices: 44.8 us -> 0.01 us  [from_neighbours(): return lax.ppermute(rows, 'seq', [(0, 1), (1, 0)])]
  transfers between devices with their start and end apart: 23 -> 8, of which waited for: 10 -> 7; matrix products, arithmetic and copies ran while one was open for 26% -> 9% of each run, Pallas kernels for 0% -> 3%
where the time goes in v1:
time: 839 us; the launch traced here: 840 us
  waiting for transfers between devices  552 us (66%)
  Pallas kernels  182 us (22%)
  local copies, waits for them, and re-layouts  65.5 us (8%)
  other arithmetic  23.9 us (3%)
  between operations  15.8 us (2%)
    unnamed x9, waiting for transfers between devices  392 us
    pallas_call x1, Pallas kernels, run_second(): pl.pallas_call(functools.partial(second_kernel, T, H), grid_spec=grid, ou...  94.6 us
    pallas_call x1, Pallas kernels, run_third(): pl.pallas_call(functools.partial(third_kernel, T, H), grid_spec=grid, out...  58.7 us
    all_gather x1, waiting for transfers between devices, shards(): early = lax.all_gather(jnp.concatenate([w_first, small]), both, axis=0)  53.7 us
    all_gather x1, waiting for transfers between devices, shards(): wt_full = lax.all_gather(w_last.T, both, axis=0, tiled=True)  38.2 us
    ppermute x2, waiting for transfers between devices, from_neighbours(): return lax.ppermute(rows, 'seq', [(0, 1), (1, 0)])  34.2 us
    all_gather x1, waiting for transfers between devices, shards(): taps_full = lax.all_gather(tap_weights, both, axis=0)  33.4 us
    pallas_call x1, Pallas kernels, run_first(): pl.pallas_call(first_kernel, grid_spec=grid, out_shape=[S((rows, D), BF)]...  29.1 us
  transfers between devices with their start and end apart: 8, of which 7 were waited for; matrix products, arithmetic and copies ran while one was open for 9% of the time, Pallas kernels for 3%

profile of v1, /device:TPU:0, one launch (start us, length us, event | category | flops | bytes accessed | tf_op | source)
XLA Modules:
  0.0 839.8 jit_solution(5727718456954227116)
XLA Ops:
  8.0 1.4 fusion.1
  16.7 53.7 %all-gather.8.cloned.1.call-done = bf16[1536,640]{1,0:T(8,128)(2,1)} async-done(((bf16[48,640]{1,0:T(8,128)(2,1)}), bf16[1536,640]{1,0:T(8,128)(2,1)}) %all-gather.8.cloned.1.call-update) | async-done | bytes 1966096 | tf_op jit(solution)/shard_map/all_gather | solution.py:520
  70.4 0.9 slice.135
  71.4 2.8 slice.134
  76.1 29.1 %first.1 = (bf16[4096,1280]{1,0:T(8,128)(2,1)}, bf16[4096,1280]{1,0:T(8,128)(2,1)}, bf16[4096,1280]{1,0:T(8,128)(2,1)}, f32[4096,128]{1,0:T(8,128)}, bf16[4096,6...) custom-call(s32[32]{0:T(128)} %get-tuple-element.115.perm, ...), custom_call_target="tpu_custom_call" | custom-call | tf_op jit(solution)/shard_map/first/pallas_call | solution.py:153
  105.2 3.5 slice.115
  112.1 33.4 %all-gather.10.cloned.1.call-done = bf16[160,40,320]{2,1,0:T(8,128)(2,1)} async-done(((bf16[5,40,320]{2,1,0:T(8,128)(2,1)}), bf16[160,40,320]{2,1,0:T(8,128)(2,1)}) %all-gather.10.cloned.1.call-update) | async-done | bytes 4096016 | tf_op jit(solution)/shard_map/all_gather | solution.py:525
  145.6 8.6 %copy.65 = bf16[16,2,5,40,320]{4,1,3,0,2:T(2,128)(2,1)} copy(bf16[16,2,5,40,320]{4,3,2,1,0:T(8,128)(2,1)} %bitcast.102) | data formatting | bytes 8192000 | tf_op jit(solution)/shard_map/reshape | solution.py:527
  154.1 10.5 %reshape.941.refs_11_.refs_7_ = bf16[3200,640]{1,0:T(8,128)(2,1)} reshape(bf16[5,16,40,2,320]{4,3,2,1,0:T(2,128)(2,1)} %bitcast.97) | data formatting | bytes 8192000 | tf_op jit(solution)/shard_map/reshape | solution.py:528
  164.7 38.2 %all-gather.6.cloned.1.call-done.refs_12_ = bf16[1280,640]{1,0:T(8,128)(2,1)} async-done(((bf16[40,640]{1,0:T(8,128)(2,1)}), bf16[1280,640]{1,0:T(8,128)(2,1)}) %all-gather.6.cloned.1.call-update) | async-done | bytes 1638416 | tf_op jit(solution)/shard_map/all_gather | solution.py:524
  203.6 0.8 copy-done.1
  204.4 94.6 %second.1 = (bf16[32,128,1280]{2,1,0:T(8,128)(2,1)}, bf16[4096,640]{1,0:T(8,128)(2,1)}, f32[640,1280]{1,0:T(8,128)}, f32[640,3200]{1,0:T(8,128)}, f32[8,1280]{1,0:T(8,128)}, /*index=5*/f32[24,640]{1,0:T(8,128)}) custom-call(s32[32]{0:T(128)} %get-tuple-element.115.perm, s32[32]{0:T(128)} %get-tuple-element.110.nval, s32[2]{0:T(128)} %pad_add_fusion.cnt, ...), custom_call_target="tpu_custom_call" | custom-call | tf_op jit(solution)/shard_map/second/pallas_call | solution.py:313
  299.1 3.6 slice.120
  303.7 1.3 convert_bitcast_fusion
  305.1 34.2 %collective-permute-done.1.refs_5_ = bf16[2048,640]{1,0:T(8,128)(2,1)} collective-permute-done((bf16[2048,640]{1,0:T(8,128)(2,1)}, bf16[2048,640]{1,0:T(8,128)(2,1)}, u32[]{:S(2)}, u32[]{:S(2)}) %collective-permute-start.1) | collective-permute-done | bytes 2621472 | tf_op jit(solution)/shard_map/ppermute | solution.py:498
  339.3 58.7 %third.1 = (bf16[32,128,1280]{2,1,0:T(8,128)(2,1)}, f32[640,1280]{1,0:T(8,128)}, f32[16,1280]{1,0:T(8,128)}, f32[24,640]{1,0:T(8,128)}) custom-call(s32[32]{0:T(128)} %get-tuple-element.115.perm, s32[32]{0:T(128)} %get-tuple-element.110.nval, s32[2]{0:T(128)} %pad_add_fusion.cnt, s32[160]{0:T(256)} %reshape.943.tab, bf16[32,128,1280]{2,1,0:T(8,128)(2,1)} %bitcast.84, ...), custom_call_target="tpu_custom_call" | custom-call | tf_op jit(solution)/shard_map/third/pallas_call | solution.py:427
  398.0 0.9 bitcast_reduce_fusion
  398.9 0.9 bitcast_reduce_fusion.2
  399.9 1.6 copy.58
  401.5 3.3 convert_bitcast_fusion.1
  404.9 5.6 convert_element_type.83
  410.5 6.8 copy.50
  417.4 11.0 %convert_element_type.84 = bf16[2,320,5,16,40]{1,0,4,3,2:T(2,128)(2,1)} reshape(bf16[640,3200]{0,1:T(8,128)(2,1)} %copy.50) | data formatting | bytes 8192000 | tf_op jit(solution)/shard_map/convert_element_type | solution.py:570
  428.4 5.2 copy.51
  433.6 147.6 %reduce-scatter.9.cloned.1.call-done = f32[80,3]{1,0:T(8,128)} async-done(((f32[2560,3]{1,0:T(8,128)}), f32[80,3]{1,0:T(8,128)}) %reduce-scatter.9.cloned.1.call-update) | async-done | bytes 976
  581.2 0.9 slice.155
  582.1 1.4 copy.61
  584.1 138.4 %all-reduce.7.cloned.1.call-done = (bf16[1280,640]{0,1:T(8,128)(2,1)}, bf16[1280,640]{0,1:T(8,128)(2,1)}) async-done(((bf16[1280,640]{0,1:T(8,128)(2,1)}, bf16[1280,640]{0,1:T(8,128)(2,1)}), (bf16[1280,640]{0,1:T(8,128)(2,1)}, bf16[1280,640]{0,1:T(8,128)(2,1)})) %all-reduce.7.cloned.1.call-update) | async-done | bytes 3276816
  722.5 1.1 convert_bitcast_fusion.2
  724.4 1.1 dynamic-slice_convert_fusion
  726.2 105.0 %reduce-scatter.11.cloned.1.call-done = bf16[1,5,40,320]{3,2,1,0:T(8,128)(2,1)} async-done(((bf16[32,5,40,320]{3,2,1,0:T(8,128)(2,1)}), bf16[1,5,40,320]{3,2,1,0:T(8,128)(2,1)}) %reduce-scatter.11.cloned.1.call-update) | async-done | bytes 128016
  831.3 1.6 bitcast_convert_fusion
  (85 shorter events, 16.1 us)
Async XLA Ops:
  7.2 63.3 %all-gather.8.cloned.1.call-start = ((), (), s32[]{:S(2)}) async-start(), calls=%async_computation.3 | async-start | bytes 2027520 | tf_op jit(solution)/shard_map/all_gather | solution.py:520
  9.4 136.1 %all-gather.10.cloned.1.call-start = ((), (), s32[]{:S(2)}) async-start(), calls=%async_computation.4 | async-start | bytes 5068800 | tf_op jit(solution)/shard_map/all_gather | solution.py:525
  10.2 192.7 %all-gather.6.cloned.1.call-start = ((), (), s32[]{:S(2)}) async-start(), calls=%async_computation.2 | async-start | bytes 1689600 | tf_op jit(solution)/shard_map/all_gather | solution.py:524
  10.9 570.3 %reduce-scatter.9.cloned.1.call-start = ((), (), s32[]{:S(2)}) async-start(), calls=%async_computation.5 | async-start | bytes 1351680
  108.7 94.2 %collective-permute-start = (bf16[2048,640]{1,0:T(8,128)(2,1)}, bf16[2048,640]{1,0:T(8,128)(2,1)S(1)}, u32[]{:S(2)}, u32[]{:S(2)}) collective-permute-start(bf16[2048,640]{1,0:T(8,128)(2,1)} %slice.115), channel_id=1, source_target_pairs={{0,1},{1,0},{2,3},{3,2},{4,5},{5,4},{6,7},{7,6},{8,9},{9,8},{10,11... | collective-permute-start | bytes 7864328 | tf_op jit(solution)/shard_map/ppermute | solution.py:498
  202.9 1.6 copy-start.1
  299.1 4.6 copy-start.3
  299.1 4.6 copy-start.2
  299.1 4.6 copy-start
  302.7 36.6 %collective-permute-start.1 = (bf16[2048,640]{1,0:T(8,128)(2,1)}, bf16[2048,640]{1,0:T(8,128)(2,1)}, u32[]{:S(2)}, u32[]{:S(2)}) collective-permute-start(bf16[2048,640]{1,0:T(8,128)(2,1)} %slice.120), channel_id=1, source_target_pairs={{0,1},{1,0},{2,3},{3,2},{4,5},{5,4},{6,7},{7,6},{8,9},{9,8},{10,11... | collective-permute-start | bytes 7864328 | tf_op jit(solution)/shard_map/ppermute | solution.py:498
  401.5 321.0 %all-reduce.7.cloned.1.call-start = ((), (), s32[]{:S(2)}) async-start(), calls=%async_computation.7 | async-start | bytes 6553600
  404.9 426.4 %reduce-scatter.11.cloned.1.call-start = ((), (), s32[]{:S(2)}) async-start(), calls=%async_computation.6 | async-start | bytes 5068800
Sparse Core Ops, SparseCore 0:
  11.5 58.9 all-gather.7
  73.3 72.2 all-gather.9
  148.4 54.4 all-gather.5
  401.6 179.5 reduce-scatter.8
  587.8 134.6 all-reduce.6
  728.1 103.1 reduce-scatter.10

commit v2 on v1

v2 whole, which is shorter than its diff:
```python
import functools
import itertools
import math

import jax
import jax.numpy as jnp
from jax import lax
from jax.experimental import pallas as pl
from jax.experimental.pallas import tpu as pltpu
from jax.sharding import PartitionSpec as P

DILATION_STEP = 128
BLOCK = 128
PACK = 4
STEP = PACK * BLOCK
CHUNK = 16
HALF = 1 / math.sqrt(2)
ROOT = 1 / math.sqrt(math.pi)
BF = jnp.bfloat16
F32 = jnp.float32
NT = (((1,), (1,)), ((), ()))
ANY = pl.BlockSpec(memory_space=pl.ANY)
SDS = jax.ShapeDtypeStruct


def dot(a, b):
    return jnp.dot(a, b, preferred_element_type=F32)


def dot_nt(a, b):
    return lax.dot_general(a, b, NT, preferred_element_type=F32)


def norm(v):
    scale = 1 / v.shape[-1]
    c = v - jnp.sum(v, -1, keepdims=True) * scale
    r = lax.rsqrt(jnp.sum(c * c, -1, keepdims=True) * scale + 1e-5)
    return c * r, r


def act(hat, gain, beta):
    z = hat * (gain * HALF) + beta * HALF
    twice = 1.0 + lax.erf(z)
    bell = z * jnp.exp2(z * z * (-1 / math.log(2)))
    return (z * HALF) * twice, (gain * 0.5) * twice + (gain * ROOT) * bell


def fold(v):
    out = v[0:8]
    for k in range(1, v.shape[0] // 8):
        out = out + v[8 * k : 8 * k + 8]
    return out


def norm_back(e, hat, r):
    scale = 1 / e.shape[-1]
    eh = e * hat
    m1 = jnp.sum(e, -1, keepdims=True) * scale
    m2 = jnp.sum(eh, -1, keepdims=True) * scale
    return (e - m1 - hat * m2) * r, eh


def over_rows(q, body):
    for at in range(0, BLOCK, CHUNK):
        body(slice(at, at + CHUNK), slice(q * BLOCK + at, q * BLOCK + at + CHUNK))


def block_rows(q):
    return slice(q * BLOCK, (q + 1) * BLOCK)


def live_rows(s, count):
    return (s.start + lax.broadcasted_iota(jnp.int32, (CHUNK, 1), 0) < count).astype(F32)


def put_row(v):
    return jnp.broadcast_to(v, (v.shape[0], 128))


def place(span):
    i = pl.program_id(0) + span[0]
    return i, pl.program_id(0) == 0, i < span[1]


def compact_spec(width, steps, writes=False):
    def where(i, perm, nval, span, *_):
        inside = jnp.minimum(i + span[0], span[1] - 1)
        return (jnp.where(span[1] > span[0], inside, steps if writes else 0), 0)

    return pl.BlockSpec((STEP, width), where)


def block_specs(width, end, steps):
    def spec(q):
        def where(i, perm, nval, span, *_):
            i = jnp.clip(i + span[0], 0, jnp.maximum(span[end] - 1, 0))
            return (perm[jnp.minimum(i, steps - 1) * PACK + q], 0, 0)

        return pl.BlockSpec((1, BLOCK, width), where)

    return [spec(q) for q in range(PACK)]


def whole(shape):
    return pl.BlockSpec(shape, lambda *_: (0,) * len(shape), pipeline_mode=pl.Buffered(1))


def vmem(shape):
    return pl.BlockSpec(shape, lambda *_: (0,) * len(shape))


def params(mb=56):
    return pltpu.CompilerParams(vmem_limit_bytes=mb * 2**20)


def cost(us):
    return pl.CostEstimate(flops=int(us * 0.9e9), bytes_accessed=1 << 20, transcendentals=0)


def first_kernel(few, perm, nval, span, *refs):
    x = refs[:PACK]
    w, vecs = refs[PACK : PACK + 2]
    act1, hat1, d1, r1, act2, hat2, d2, r2, edge, mid = refs[PACK + 2 :]
    i, _, busy = place(span)
    D, I = w.shape
    one, two = slice(0, D), slice(D, D + I)

    @pl.when(busy)
    def _():
        def rows_first(q):
            def rows(s, t):
                hat, r = norm(x[q][0, s, :].astype(F32))
                a, d = act(hat, vecs[0:1, one], vecs[1:2, one])
                act1[t, :] = a.astype(BF)
                hat1[t, :] = hat.astype(BF)
                d1[t, :] = d.astype(BF)
                r1[t, :] = put_row(r)

            over_rows(q, rows)

        def rows_second(q):
            def rows(s, t):
                hat, r = norm(mid[t, :] + vecs[2:3, two])
                a, d = act(hat, vecs[0:1, two], vecs[1:2, two])
                live = live_rows(s, nval[i * PACK + q])
                act2[t, :] = (a * live).astype(BF)
                hat2[t, :] = hat.astype(BF)
                d2[t, :] = (d * live).astype(BF)
                r2[t, :] = put_row(r)

            over_rows(q, rows)

        rows_first(0)
        for q in range(PACK):
            mid[block_rows(q), :] = dot(act1[block_rows(q), :], w[...])
            if q + 1 < PACK:
                rows_first(q + 1)
            if q:
                rows_second(q - 1)
        rows_second(PACK - 1)

    @pl.when(i < few)
    def _():
        edge[...] = act2[...]


def edge_spec(width, few):
    return pl.BlockSpec((STEP, width), lambda i, *_: (jnp.minimum(i, few - 1), 0))


def run_first(perm, nval, span, x, w, vecs, few):
    T, _, D = x.shape
    I = w.shape[1]
    steps = T // PACK
    rows = (steps + 1) * STEP
    widths = (D, D, D, 128, I, I, I, 128)
    kinds = (BF, BF, BF, F32, BF, BF, BF, F32)
    grid = pltpu.PrefetchScalarGridSpec(
        num_scalar_prefetch=3,
        grid=(steps,),
        in_specs=block_specs(D, 1, steps) + [whole(w.shape), whole(vecs.shape)],
        out_specs=[compact_spec(v, steps, True) for v in widths] + [edge_spec(I, few)],
        scratch_shapes=[pltpu.VMEM((STEP, I), F32)],
    )
    return pl.pallas_call(
        functools.partial(first_kernel, few),
        grid_spec=grid,
        out_shape=[SDS((rows, v), k) for v, k in zip(widths, kinds)] + [SDS((few * STEP, I), BF)],
        compiler_params=params(),
        cost_estimate=cost(30),
        name="first",
    )(perm, nval, span, *([x] * PACK), w, vecs)


def gather_taps(tab, step, slot, im, local, halo, zero, sems, T, H, width):
    for q in range(PACK):
        for k in range(im.shape[2] // width):
            code = tab[(step * PACK + q) * (im.shape[2] // width) + k]
            dst = im.at[slot, pl.ds(q * BLOCK, BLOCK), pl.ds(k * width, width)]

            @pl.when(code < T)
            def _(code=code, dst=dst):
                src = local.at[pl.ds(pl.multiple_of(code * BLOCK, BLOCK), BLOCK), :]
                pltpu.make_async_copy(src, dst, sems.at[slot]).start()

            if H:

                @pl.when((code >= T) & (code < T + H))
                def _(code=code, dst=dst):
                    src = halo.at[pl.ds(pl.multiple_of((code - T) * BLOCK, BLOCK), BLOCK), :]
                    pltpu.make_async_copy(src, dst, sems.at[slot]).start()

            @pl.when(code >= T + H)
            def _(dst=dst):
                pltpu.make_async_copy(zero, dst, sems.at[slot]).start()


def wait_slot(buf, slot, sems):
    pltpu.make_async_copy(buf.at[slot], buf.at[slot], sems.at[slot]).wait()


def put_blocks(perm, i, slot, obuf, out, osem, span):
    for q in range(PACK):
        pltpu.make_async_copy(obuf.at[slot, q], out.at[perm[i * PACK + q]], osem.at[slot]).start()

    @pl.when(i == span[2] - 1)
    def _():
        wait_slot(obuf, slot, osem)

        @pl.when(i > span[0])
        def _():
            wait_slot(obuf, 1 - slot, osem)


def second_kernel(T, H, skip, perm, nval, span, tab, *refs):
    x = refs[:PACK]
    c = refs[PACK : 2 * PACK]
    local, halo, zero, taps, wt, vecs = refs[2 * PACK : 2 * PACK + 6]
    out, gms, act3, gb, sum_i, *rest = refs[2 * PACK + 6 + skip :]
    edge = rest.pop(0) if H else None
    im, mid, back, hat3, d3, r3, br, obuf, sems, osem = rest
    i, begins, busy = place(span)
    D, I = wt.shape
    one, three = slice(0, D), slice(D + I, D + 2 * I)
    slot = lax.rem(i, 2)

    @pl.when(begins)
    def _():
        sum_i[...] = jnp.zeros_like(sum_i)

    @pl.when((i >= span[0] + 2) & (i < span[2]))
    def _():
        wait_slot(obuf, slot, osem)

    @pl.when(busy)
    def _():
        @pl.when(begins)
        def _():
            gather_taps(tab, i, slot, im, local, halo, zero, sems, T, H, I)

        @pl.when(i + 1 < span[1])
        def _():
            gather_taps(tab, i + 1, 1 - slot, im, local, halo, zero, sems, T, H, I)

        def products(q):
            def rows(s, t):
                live = live_rows(s, nval[i * PACK + q])
                gb[t, :] = (c[q][0, s, :].astype(F32) * live).astype(BF)

            over_rows(q, rows)
            mid[block_rows(q), :] = dot(im[slot, block_rows(q), :], taps[...])
            back[block_rows(q), :] = dot(gb[block_rows(q), :], wt[...])

        def rows_third(q):
            def rows(s, t):
                hat, r = norm(mid[t, :] + vecs[2:3, three])
                a, d = act(hat, vecs[0:1, three], vecs[1:2, three])
                act3[t, :] = a.astype(BF)
                hat3[t, :] = hat.astype(BF)
                d3[t, :] = d.astype(BF)
                r3[t, :] = put_row(r)

            over_rows(q, rows)

        def rows_out(q):
            def rows(s, t):
                live = live_rows(s, nval[i * PACK + q])
                v = x[q][0, s, :].astype(F32) + live * (br[t, :] + vecs[2:3, one])
                obuf[slot, q, s, :] = v.astype(BF)

            over_rows(q, rows)

        def rows_back(q):
            def rows(s, t):
                hat = hat3[t, :].astype(F32)
                e = back[t, :] * d3[t, :].astype(F32)
                g, eh = norm_back(e, hat, r3[t, 0:1])
                g = g.astype(BF)
                gms[t, :] = g
                sum_i[0:8, :] += fold(eh)
                sum_i[8:16, :] += fold(e)
                sum_i[16:24, :] += fold(g.astype(F32))

            over_rows(q, rows)

        wait_slot(im, slot, sems)
        products(0)
        for q in range(PACK):
            if q + 1 < PACK:
                products(q + 1)
            rows_third(q)
            br[block_rows(q), :] = dot_nt(act3[block_rows(q), :], wt[...])
            rows_back(q)
            rows_out(q)
        if H:
            edge[...] = gms[...]

    @pl.when((i >= span[1]) & (i < span[2]))
    def _():
        for q in range(PACK):
            obuf[slot, q] = x[q][0]

    @pl.when(i < span[2])
    def _():
        put_blocks(perm, i, slot, obuf, out, osem, span)


def run_second(perm, nval, span, tab, x, cot, local, halo, zero, taps, wt, vecs, most, old=(), pins=()):
    T, _, D = x.shape
    I = wt.shape[1]
    steps = T // PACK
    rows = (steps + 1) * STEP
    H = 0 if halo is None else halo.shape[0] // BLOCK
    halo = zero if halo is None else halo
    V = pltpu.VMEM
    grid = pltpu.PrefetchScalarGridSpec(
        num_scalar_prefetch=4,
        grid=(most,),
        in_specs=block_specs(D, 2, steps)
        + block_specs(D, 1, steps)
        + [ANY, ANY, ANY, whole(taps.shape), whole(wt.shape), whole(vecs.shape)]
        + [ANY] * len((*old, *pins)),
        out_specs=[ANY]
        + [compact_spec(v, steps, True) for v in (I, I, D)]
        + [vmem((24, I))]
        + [edge_spec(I, most)] * (H > 0),
        scratch_shapes=[
            V((2, STEP, taps.shape[0]), BF),
            V((STEP, I), F32),
            V((STEP, I), F32),
            V((STEP, I), BF),
            V((STEP, I), BF),
            V((STEP, 128), F32),
            V((STEP, D), F32),
            V((2, PACK, BLOCK, D), BF),
            pltpu.SemaphoreType.DMA((2,)),
            pltpu.SemaphoreType.DMA((2,)),
        ],
    )
    return pl.pallas_call(
        functools.partial(second_kernel, T, H, len((*old, *pins))),
        grid_spec=grid,
        out_shape=[
            SDS((T, BLOCK, D), BF),
            SDS((rows, I), BF),
            SDS((rows, I), BF),
            SDS((rows, D), BF),
            SDS((24, I), F32),
        ]
        + [SDS((most * STEP, I), BF)] * (H > 0),
        input_output_aliases={10 + 2 * PACK + k: k for k in range(len(old))},
        compiler_params=params(),
        cost_estimate=cost(40),
        name="second",
    )(perm, nval, span, tab, *([x] * PACK), *([cot] * PACK), local, halo, zero, taps, wt, vecs, *old, *pins)


def turn(total, put):
    width = total.shape[0] // 128 * 128
    for at in range(0, total.shape[1], width):
        put(at, total[0:width, at : at + width].T)


def parts(at, v, form, part):
    Z, X, C, Y = form
    size = min(part, v.shape[0])
    for n in range(0, v.shape[0], size):
        d, row = divmod(at + n, part)
        digits = (d // (X * C * Y), d // (C * Y) % X, d // Y % C, d % Y)
        yield digits, slice(row, row + size), v[n : n + size]


def by_core(core, groups, keep, send):
    if groups == 1:
        return lambda c, at, v: keep.__setitem__(at, v)

    def put(c, at, v):
        @pl.when(core == c)
        def _():
            keep[at] = v

        @pl.when(core != c)
        def _():
            send[at] = v.astype(BF)

    return put


def weights_kernel(T, H, form, perm, nval, span, tab, core, *refs):
    gms, act3, gb, local, halo, zero = refs[:6]
    taps_t, taps_s, last_t, last_s, sum_d = refs[6:11]
    im, glast, gtaps, sems = refs[11:]
    i, begins, busy = place(span)
    I = gms.shape[1]
    slot = lax.rem(i, 2)

    @pl.when(begins)
    def _():
        glast[...] = jnp.zeros_like(glast)
        gtaps[...] = jnp.zeros_like(gtaps)

    @pl.when(busy)
    def _():
        @pl.when(begins)
        def _():
            gather_taps(tab, i, slot, im, local, halo, zero, sems, T, H, I)

        @pl.when(i + 1 < span[1])
        def _():
            gather_taps(tab, i + 1, 1 - slot, im, local, halo, zero, sems, T, H, I)

        ones = jnp.ones((16, STEP), BF)
        glast[...] += dot(jnp.concatenate([act3[...].T, ones]), gb[...])
        wait_slot(im, slot, sems)
        gtaps[...] += dot(gms[...].T, im[slot])

    @pl.when(pl.program_id(0) == pl.num_programs(0) - 1)
    def _():
        sum_d[...] = glast[I : I + 8, :]
        Z, X, C, Y = form
        rows = I // (Z * X * C)

        def put_taps(at, v):
            put = by_core(core[0], C, taps_t, taps_s)
            for z, x, c in itertools.product(range(Z), range(X), range(C)):
                b = (z * X + x) * C + c
                put(c, (x, z, at // I), v[b * rows : (b + 1) * rows])

        def put_last(at, v):
            put = by_core(core[0], C, last_t, last_s)
            for (z, x, c, y), rows, piece in parts(at, v, form, last_t.shape[-2]):
                put(c, (z, x * Y + y, rows), piece)

        turn(gtaps, put_taps)
        turn(glast, put_last)


def run_weights(perm, nval, span, tab, core, gms, act3, gb, local, halo, zero, form):
    D, I = gb.shape[1], gms.shape[1]
    T = perm.shape[0]
    steps = T // PACK
    taps = tab.shape[0] // T
    H = halo.shape[0] // BLOCK
    V = pltpu.VMEM
    Z, X, C, Y = form
    a = (X, Z, taps, I // (Z * X * C), I)
    b = (Z, X * Y, D // (Z * X * C * Y), I)
    grid = pltpu.PrefetchScalarGridSpec(
        num_scalar_prefetch=5,
        grid=(steps,),
        in_specs=[compact_spec(v, steps) for v in (I, I, D)] + [ANY, ANY, ANY],
        out_specs=[whole(a), whole(a), whole(b), whole(b), whole((8, D))],
        scratch_shapes=[
            V((2, STEP, taps * I), BF),
            V((I + 16, D), F32),
            V((I, taps * I), F32),
            pltpu.SemaphoreType.DMA((2,)),
        ],
    )
    return pl.pallas_call(
        functools.partial(weights_kernel, T, H, form),
        grid_spec=grid,
        out_shape=[SDS(a, F32), SDS(a, BF), SDS(b, F32), SDS(b, BF), SDS((8, D), F32)],
        compiler_params=params(),
        cost_estimate=cost(40),
        name="weights",
    )(perm, nval, span, tab, core, gms, act3, gb, local, halo, zero)


def third_kernel(T, H, skip, form, perm, nval, span, tab, core, *refs):
    local, halo, zero, taps, act1, hat2, d2, r2 = refs[:8]
    gmf, first_t, first_s, sum_i = refs[8 + skip : 12 + skip]
    im, mid, gfirst, sems = refs[12 + skip :]
    i, begins, busy = place(span)
    I = taps.shape[1]
    slot = lax.rem(i, 2)

    @pl.when(begins)
    def _():
        gfirst[...] = jnp.zeros_like(gfirst)
        sum_i[...] = jnp.zeros_like(sum_i)

    @pl.when(busy)
    def _():
        @pl.when(begins)
        def _():
            gather_taps(tab, i, slot, im, local, halo, zero, sems, T, H, I)

        @pl.when(i + 1 < span[1])
        def _():
            gather_taps(tab, i + 1, 1 - slot, im, local, halo, zero, sems, T, H, I)

        wait_slot(im, slot, sems)

        def product(q):
            total = 0
            for k in range(taps.shape[0] // I):
                s = slice(k * I, (k + 1) * I)
                total = total + dot_nt(im[slot, block_rows(q), s], taps[s, :])
            mid[block_rows(q), :] = total

        def rows_second(q):
            def rows(s, t):
                hat = hat2[t, :].astype(F32)
                e = mid[t, :] * d2[t, :].astype(F32)
                g, eh = norm_back(e, hat, r2[t, 0:1])
                g = g.astype(BF)
                gmf[t, :] = g
                sum_i[0:8, :] += fold(eh)
                sum_i[8:16, :] += fold(e)
                sum_i[16:24, :] += fold(g.astype(F32))

            over_rows(q, rows)

        product(0)
        for q in range(PACK):
            if q + 1 < PACK:
                product(q + 1)
            rows_second(q)
        gfirst[...] += dot(gmf[...].T, act1[...])

    @pl.when(pl.program_id(0) == pl.num_programs(0) - 1)
    def _():
        Z, X, C, Y = form

        def put_first(at, v):
            put = by_core(core[0], C, first_t, first_s)
            for (z, x, c, y), rows, piece in parts(at, v, form, first_t.shape[-2]):
                put(c, (x * Y + y, z, rows), piece)

        turn(gfirst, put_first)


def run_third(perm, nval, span, tab, core, local, halo, zero, taps, saved, form, pins=()):
    act1, hat1, d1, r1, act2, hat2, d2, r2 = saved
    T = perm.shape[0]
    D, I = act1.shape[1], act2.shape[1]
    steps = T // PACK
    rows = (steps + 1) * STEP
    H = halo.shape[0] // BLOCK
    V = pltpu.VMEM
    Z, X, C, Y = form
    a = (X * Y, Z, D // (Z * X * C * Y), I)
    grid = pltpu.PrefetchScalarGridSpec(
        num_scalar_prefetch=5,
        grid=(steps,),
        in_specs=[ANY, ANY, ANY, whole(taps.shape)]
        + [compact_spec(v, steps) for v in (D, I, I, 128)]
        + [ANY] * len(pins),
        out_specs=[compact_spec(I, steps, True), whole(a), whole(a), vmem((24, I))],
        scratch_shapes=[
            V((2, STEP, taps.shape[0]), BF),
            V((STEP, I), F32),
            V((I, D), F32),
            pltpu.SemaphoreType.DMA((2,)),
        ],
    )
    return pl.pallas_call(
        functools.partial(third_kernel, T, H, len(pins), form),
        grid_spec=grid,
        out_shape=[SDS((rows, I), BF), SDS(a, F32), SDS(a, BF), SDS((24, I), F32)],
        compiler_params=params(),
        cost_estimate=cost(40),
        name="third",
    )(perm, nval, span, tab, core, local, halo, zero, taps, act1, hat2, d2, r2, *pins)


def spread_kernel(n_old, skip, perm, nval, span, *refs):
    c = refs[:PACK]
    gmf, hat1, d1, r1, w = refs[PACK : PACK + 5]
    before = refs[PACK + 6] if n_old else None
    gin, sum_d = refs[PACK + 5 + skip : PACK + 7 + skip]
    big, obuf, osem = refs[PACK + 7 + skip :]
    i, begins, busy = place(span)
    slot = lax.rem(i, 2)

    @pl.when(begins)
    def _():
        sum_d[...] = before[...] if n_old else jnp.zeros_like(sum_d)

    @pl.when((i >= span[0] + 2) & (i < span[2]))
    def _():
        wait_slot(obuf, slot, osem)

    @pl.when(busy)
    def _():
        def product(q):
            big[block_rows(q), :] = dot_nt(gmf[block_rows(q), :], w[...])

        def rows_first(q):
            def rows(s, t):
                hat = hat1[t, :].astype(F32)
                e = big[t, :] * d1[t, :].astype(F32)
                g, eh = norm_back(e, hat, r1[t, 0:1])
                obuf[slot, q, s, :] = (c[q][0, s, :].astype(F32) + g).astype(BF)
                sum_d[0:8, :] += fold(eh)
                sum_d[8:16, :] += fold(e)

            over_rows(q, rows)

        product(0)
        for q in range(PACK):
            if q + 1 < PACK:
                product(q + 1)
            rows_first(q)

    @pl.when((i >= span[1]) & (i < span[2]))
    def _():
        for q in range(PACK):
            obuf[slot, q] = c[q][0]

    @pl.when(i < span[2])
    def _():
        put_blocks(perm, i, slot, obuf, gin, osem, span)


def run_spread(perm, nval, span, cot, gmf, hat1, d1, r1, w, most, old=(), pins=()):
    T, _, D = cot.shape
    I = w.shape[1]
    steps = T // PACK
    V = pltpu.VMEM
    grid = pltpu.PrefetchScalarGridSpec(
        num_scalar_prefetch=3,
        grid=(most,),
        in_specs=block_specs(D, 2, steps)
        + [compact_spec(v, steps) for v in (I, D, D, 128)]
        + [whole(w.shape)]
        + [ANY, vmem((16, D))][: len(old)]
        + [ANY] * len(pins),
        out_specs=[ANY, vmem((16, D))],
        scratch_shapes=[
            V((STEP, D), F32),
            V((2, PACK, BLOCK, D), BF),
            pltpu.SemaphoreType.DMA((2,)),
        ],
    )
    return pl.pallas_call(
        functools.partial(spread_kernel, len(old), len((*old, *pins))),
        grid_spec=grid,
        out_shape=[SDS((T, BLOCK, D), BF), SDS((16, D), F32)],
        input_output_aliases={8 + PACK: 0} if old else {},
        compiler_params=params(),
        cost_estimate=cost(12),
        name="spread",
    )(perm, nval, span, *([cot] * PACK), gmf, hat1, d1, r1, w, *old, *pins)


ORDER = ("z", "x", "c", "y")


def digit_sizes():
    return {"z": lax.axis_size("batch") // 4, "x": 2, "c": 2, "y": lax.axis_size("seq")}


def own_digits(sizes):
    b = lax.axis_index("batch")
    return {"z": b // 4, "x": (b // 2) % 2, "c": b % 2, "y": lax.axis_index("seq")}


def flat(digits, names, sizes):
    out = 0
    for n, d in zip(names, digits):
        out = out * sizes[n] + d
    return out


def offsets(names, sizes):
    return list(itertools.product(*[range(sizes[n]) for n in names]))


def move(value, names, off, sizes):
    pairs = []
    for device in itertools.product(*[range(sizes[n]) for n in ORDER]):
        target = list(device)
        for n, o in zip(names, off):
            at = ORDER.index(n)
            target[at] = (target[at] + o) % sizes[n]
        pairs.append((flat(device, ORDER, sizes), flat(target, ORDER, sizes)))
    return lax.ppermute(value, ("batch", "seq"), pairs)


def gather_over(value, names, sizes):
    return jnp.stack([move(value, names, off, sizes) if any(off) else value for off in offsets(names, sizes)])


def gather_part(value, sizes):
    return gather_over(gather_over(value, ("z",), sizes), ("x", "y"), sizes)


def back_index(sizes, own):
    z = (own["z"] - jnp.arange(sizes["z"])) % sizes["z"]
    x = (own["x"] - jnp.arange(2)) % 2
    y = (own["y"] - jnp.arange(sizes["y"])) % sizes["y"]
    place = (x[None, :, None] * sizes["y"] + y[None, None, :]) * sizes["z"] + z[:, None, None]
    return place.astype(jnp.int32).reshape(-1)


def reduce_over(terms, names, sizes, own, kind=BF):
    me = [own[n] for n in names]

    def piece(off):
        at = flat([(d + o) % sizes[n] for n, d, o in zip(names, me, off)], names, sizes)
        total = 0
        for t in terms:
            total = total + lax.dynamic_index_in_dim(t, at, 0, keepdims=False).astype(F32)
        return total.astype(kind if any(off) else F32)

    offs = offsets(names, sizes)
    return [piece(offs[0])] + [move(piece(off), names, off, sizes) for off in offs[1:]]


def add_up(terms):
    total = terms[0].astype(F32)
    for t in terms[1:]:
        total = total + t.astype(F32)
    return total


def reduce_small(v, sizes, own):
    z, x, c, y = (sizes[n] for n in ORDER)
    n = v.shape[0]
    v = v.reshape(n, z, x, c, y, -1).transpose(3, 2, 4, 1, 0, 5)
    m = v.shape[-1]
    terms = reduce_over([v.reshape(c, x * y, z, n, m)], ("c",), sizes, own, F32)
    terms = reduce_over(terms, ("x", "y"), sizes, own, F32)
    return add_up(reduce_over(terms, ("z",), sizes, own, F32))


def tall(n):
    return -(-n // 16) * 16


def pack_early(w_first, norm_gain, shift_params):
    small = jnp.concatenate([norm_gain[None], shift_params]).reshape(1, -1)
    return jnp.concatenate([w_first, jnp.pad(small, ((0, 7), (0, w_first.shape[1] - small.shape[1])))])


def early_kernel(n_batch, rows, part, at, core, own, other, held, w, vecs, sheet):
    def go(first, second):
        for b in range(0, n_batch, 2):
            for c, src in ((0, first), (1, second)):
                both = []
                for y in range(2):
                    chunk = src[at[b + y]].astype(F32)
                    both.append(chunk[:rows])
                    d = 2 * (b + c) + y
                    sheet[d : d + 1, :] = chunk[rows : rows + 1, :]
                w[2 * rows * (b + c) : 2 * rows * (b + c + 1), :] = jnp.concatenate(both).astype(BF)

    @pl.when(core[0] == 0)
    def _():
        go(own, other)

    @pl.when(core[0] != 0)
    def _():
        go(other, own)

    width = vecs.shape[1]
    column = lax.broadcasted_iota(jnp.int32, (1, width), 1).astype(F32)
    owner = jnp.floor((column + 0.5) * (1 / part))
    rest = column - owner * part
    pick = (lax.broadcasted_iota(jnp.int32, (part, width), 0).astype(F32) == rest).astype(BF)
    mine = (lax.broadcasted_iota(jnp.int32, (2 * n_batch, width), 0).astype(F32) == owner).astype(F32)
    vecs[...] = jnp.zeros_like(vecs)
    for k in range(3):
        spread = dot(sheet[:, k * part : (k + 1) * part].astype(BF), pick)
        vecs[k : k + 1, :] = jnp.sum(spread * mine, axis=0, keepdims=True)


def run_early(at, core, own, other, rows, part, held):
    n_batch = own.shape[0]
    width = 2 * n_batch * part
    lanes = own.shape[-1]
    smem, v = pl.BlockSpec(memory_space=pltpu.SMEM), pl.BlockSpec(memory_space=pltpu.VMEM)
    return pl.pallas_call(
        functools.partial(early_kernel, n_batch, rows, part),
        in_specs=[smem, smem, v, v, ANY],
        out_specs=[v, v],
        out_shape=[SDS((2 * n_batch * rows, lanes), BF), SDS((8, width), F32)],
        scratch_shapes=[pltpu.VMEM((2 * n_batch, lanes), F32)],
        compiler_params=params(),
        cost_estimate=cost(4),
        name="early",
    )(at, core, own, other, held)


def pack_late(tap_weights, w_last):
    taps, rows, lanes = tap_weights.shape
    flat_taps = tap_weights.reshape(taps * rows, lanes)
    top = late_cut(taps * rows)
    low = jnp.pad(flat_taps[top:], ((0, 2 * top - taps * rows), (0, 0)))
    return jnp.concatenate([jnp.concatenate([flat_taps[:top], low], axis=1), w_last.T])


def late_cut(rows):
    return -(-(rows + 1) // 16) * 8


def late_kernel(n_batch, taps, rows, at, core, own, other, full, wt):
    lanes = own.shape[-1]
    half = lanes // 2
    top = late_cut(taps * rows)
    left = lax.broadcasted_iota(jnp.int32, (1, lanes), 1) < half

    def go(first, second):
        def step(zx, carry):
            done = []
            for src in (first, second):
                one = src[at[2 * zx]].astype(F32)
                two = src[at[2 * zx + 1]].astype(F32)
                upper = jnp.where(left, one[:top], pltpu.roll(two[:top], half, axis=1))
                lower = jnp.where(left, pltpu.roll(one[:top], half, axis=1), two[:top])
                done.append(jnp.concatenate([upper, lower]))
                c = len(done) - 1
                here = pl.ds(pl.multiple_of((2 * zx + c) * 2 * rows, 16), 2 * rows)
                wt[here, :] = jnp.concatenate([one[top:], two[top:]]).astype(BF)
            for k in range(taps):
                s = slice(k * rows, (k + 1) * rows)
                here = pl.ds(pl.multiple_of(k * n_batch * rows + zx * 2 * rows, 16), 2 * rows)
                full[here, :] = jnp.concatenate([done[0][s], done[1][s]]).astype(BF)
            return carry

        lax.fori_loop(0, n_batch // 2, step, 0)

    @pl.when(core[0] == 0)
    def _():
        go(own, other)

    @pl.when(core[0] != 0)
    def _():
        go(other, own)


def run_late(at, core, own, other, taps, rows):
    n_batch = own.shape[0]
    lanes = own.shape[-1]
    smem, v = pl.BlockSpec(memory_space=pltpu.SMEM), pl.BlockSpec(memory_space=pltpu.VMEM)
    return pl.pallas_call(
        functools.partial(late_kernel, n_batch, taps, rows),
        in_specs=[smem, smem, v, v],
        out_specs=[v, v],
        out_shape=[SDS((taps * n_batch * rows, lanes), BF), SDS((2 * n_batch * rows, lanes), BF)],
        compiler_params=params(),
        cost_estimate=cost(7),
        name="late",
    )(at, core, own, other)


def gather_weights(w_first, tap_weights, w_last, norm_gain, shift_params):
    sizes = digit_sizes()
    own = own_digits(sizes)
    at = back_index(sizes, own)
    core = own["c"].reshape(1).astype(jnp.int32)
    part = norm_gain.shape[0]
    taps, rows, _ = tap_weights.shape

    early, late = pack_early(w_first, norm_gain, shift_params), pack_late(tap_weights, w_last)
    line = gather_over(early, ("z",), sizes)
    line, late = lax.optimization_barrier((line, late))
    held = gather_over(late, ("z",), sizes)
    mine = gather_over(line, ("x", "y"), sizes).reshape(-1, *early.shape)
    other = move(mine, ("c",), (1,), sizes)
    w, vecs = run_early(at, core, mine, other, w_first.shape[0], part, held)
    mine = gather_over(held, ("x", "y"), sizes).reshape(-1, *late.shape)
    other = move(mine, ("c",), (1,), sizes)
    full, wt = run_late(at, core, mine, other, taps, rows)
    return w, full, wt, vecs


class Shares:
    def __init__(self, taps):
        self.sizes = digit_sizes()
        self.own = own_digits(self.sizes)
        self.taps = taps
        self.terms = {}

    def step(self, name, *names):
        self.terms[name] = reduce_over(self.terms[name], names, self.sizes, self.own)

    def start(self, name, keep, send):
        self.terms[name] = [keep, move(send, ("c",), (1,), self.sizes)]

    def hold(self, names, *others):
        held = [self.terms[name] for name in names]
        held, _ = lax.optimization_barrier((held, others))
        self.terms.update(zip(names, held))

    def own_part(self, *names):
        return [self.terms[name][0] for name in names]

    def finish_taps(self):
        y = self.sizes["y"]
        v = add_up(self.terms["taps"])
        lanes = v.shape[-1]
        v = v.reshape(-1, y, lanes // y).transpose(1, 0, 2)
        v = add_up(reduce_over([v], ("y",), self.sizes, self.own))
        return v.reshape(self.taps, -1, lanes // y)

    def finish(self, name):
        return add_up(self.terms[name])


def gather_weights_plainly(w_first, tap_weights, w_last, norm_gain, shift_params):
    both = ("batch", "seq")
    taps, rows, lanes = tap_weights.shape
    n_batch, n_seq = lax.axis_size("batch"), lax.axis_size("seq")
    w = lax.all_gather(w_first, both, axis=0, tiled=True)
    wt = lax.all_gather(w_last.T, both, axis=0, tiled=True)
    full = lax.all_gather(tap_weights, both, axis=0).reshape(n_batch, n_seq, taps, rows, lanes)
    full = full.transpose(2, 0, 3, 1, 4).reshape(taps * n_batch * rows, n_seq * lanes)
    vecs = lax.all_gather(jnp.concatenate([norm_gain[None], shift_params]), both, axis=1, tiled=True)
    return w, full, wt, jnp.pad(vecs.astype(F32), ((0, 5), (0, 0)))


def reduce_plainly(taps_t, last_t, first_t, sums):
    both = ("batch", "seq")
    n_batch, n_seq = lax.axis_size("batch"), lax.axis_size("seq")
    taps, rows, lanes = taps_t.shape[2:]
    a = taps_t.reshape(taps, n_batch, -1, n_seq, lanes // n_seq).transpose(1, 3, 0, 2, 4)
    a = a.reshape(n_batch * n_seq, taps, -1, lanes // n_seq).astype(F32)
    a = lax.psum_scatter(a, both, scatter_dimension=0)
    b = lax.psum_scatter(last_t.reshape(-1, lanes).astype(F32), both, scatter_dimension=0, tiled=True).T
    f = lax.psum_scatter(first_t.reshape(-1, lanes).astype(F32), both, scatter_dimension=0, tiled=True)
    s = lax.psum_scatter(sums, both, scatter_dimension=1, tiled=True)
    return a, b, f, s


def layout_tables(lens, seq_index, n_seq, nblk, reach):
    count = lens.shape[0] * nblk
    edge = edge_blocks(lens.shape[0], n_seq, nblk, reach)
    t = jnp.arange(count, dtype=jnp.int32)
    s, j = t // nblk, t % nblk
    length = jnp.repeat(lens, nblk, total_repeat_length=count)

    def ranks(index):
        live = (index * nblk + j) * BLOCK < length
        reads_left = (j < reach) & (index > 0)
        reads_right = (j >= nblk - reach) & (index < n_seq - 1)
        reads_right = reads_right & ((index + 1) * nblk * BLOCK < length)
        kind = jnp.where(live, jnp.where(reads_left | reads_right, 0, 1), 2)
        key = kind * count + t
        rank = jnp.sum((key[None, :] < key[:, None]).astype(jnp.int32), axis=1)
        return rank, kind

    rank, kind = ranks(seq_index)
    chosen = (rank[:, None] == t[None, :]).astype(jnp.int32)
    perm = jnp.sum(chosen * t[:, None], axis=0)
    left = jnp.clip(length - (seq_index * nblk + j) * BLOCK, 0, BLOCK)
    nval = jnp.sum(chosen * left[:, None], axis=0)
    cnt = jnp.stack(
        [
            (jnp.sum((kind == 0).astype(jnp.int32)) + PACK - 1) // PACK,
            (jnp.sum((kind < 2).astype(jnp.int32)) + PACK - 1) // PACK,
        ]
    )
    hops = hop_list(n_seq, nblk, reach)
    zero = count + (1 if n_seq == 2 else len(hops)) * edge
    code = []
    for k in range(-reach, reach + 1):
        far = seq_index * nblk + j + k
        inside = (kind < 2) & (far >= 0) & (far * BLOCK < length)
        place = jnp.full_like(t, zero)
        for hop in [0] + hops:
            other = seq_index + hop
            at = rank if hop == 0 else ranks(other)[0]
            there = far - other * nblk
            mine = inside & (there >= 0) & (there < nblk)
            found = jnp.sum(
                jnp.where((s * nblk + there)[:, None] == t[None, :], at[None, :], 0), axis=1
            )
            base = 0 if hop == 0 else count + (0 if n_seq == 2 else hops.index(hop) * edge)
            place = jnp.where(mine, base + found, place)
        code.append(place)
    code = jnp.stack(code, axis=1)
    code = jnp.sum(chosen[:, :, None] * code[:, None, :], axis=0)
    return (perm, nval, cnt), code.reshape(-1), code[:, ::-1].reshape(-1)


def edge_blocks(seqs, n_seq, nblk, reach):
    return seqs * min(nblk, reach * (1 if n_seq == 2 else 2))


def hop_list(n_seq, nblk, reach):
    furthest = min(n_seq - 1, -(-reach // nblk))
    return [hop for h in range(1, furthest + 1) for hop in (h, -h)]


def from_neighbours(rows, n_seq, hops):
    if n_seq == 2:
        return lax.ppermute(rows, "seq", [(0, 1), (1, 0)])
    parts = [
        lax.ppermute(rows, "seq", [(i, i - hop) for i in range(n_seq) if 0 <= i - hop < n_seq])
        for hop in hops
    ]
    return jnp.concatenate(parts, axis=0) if parts else rows[:0]


def shards(inputs, cotangent, lengths, w_first, tap_weights, w_last, norm_gain, shift_params):
    n_batch = lax.axis_size("batch")
    n_seq = lax.axis_size("seq")
    seq_index = lax.axis_index("seq")
    both = ("batch", "seq")
    micro, seqs, span, D = inputs.shape
    I = w_first.shape[1]
    K = tap_weights.shape[0]
    nblk = span // BLOCK
    T = micro * seqs * nblk
    reach = K // 2
    direct = n_seq == 2 and n_batch % 4 == 0 and w_first.shape[0] % 8 == 0
    gather = gather_weights if direct else gather_weights_plainly
    w_full, taps_full, wt_full, vecs = gather(w_first, tap_weights, w_last, norm_gain, shift_params)

    two, three = slice(D, D + I), slice(D + I, D + 2 * I)

    (perm, nval, cnt), ahead, back = layout_tables(
        lengths.reshape(-1), seq_index, n_seq, nblk, reach
    )
    hops = hop_list(n_seq, nblk, reach)
    edge = edge_blocks(micro * seqs, n_seq, nblk, reach) * BLOCK
    zero = jnp.zeros((BLOCK, I), BF)
    x = inputs.reshape(T, BLOCK, D)
    cot = cotangent.reshape(T, BLOCK, D)
    total, few = T // PACK, -(-edge // STEP)
    start, steps = jnp.zeros_like(cnt[0]), jnp.full_like(cnt[0], total)
    outer = (perm, nval, jnp.stack([start, cnt[0], cnt[0]]))
    inner = (perm, nval, jnp.stack([cnt[0], cnt[1], steps]))
    every = (perm, nval, jnp.stack([start, cnt[1], steps]))

    form = tuple(digit_sizes()[n] for n in ORDER) if direct else (1, 1, 1, 1)
    core = (lax.axis_index("batch") % 2).astype(jnp.int32).reshape(1)
    shares = Shares(K) if direct else None
    *saved, rim = run_first(*every, x, w_full, vecs, few)
    halo = from_neighbours(rim, n_seq, hops)
    args = (taps_full, wt_full, vecs)
    *kept, sum_third = run_second(*inner, ahead, x, cot, saved[4], None, zero, *args, total)
    out, gms, act3, gb, more, rim = run_second(
        *outer, ahead, x, cot, saved[4], halo, zero, *args, few, kept
    )
    halo_back = from_neighbours(rim, n_seq, hops)
    sum_third = sum_third + more
    taps_t, taps_s, last_t, last_s, sum_out = run_weights(
        *every, ahead, core, gms, act3, gb, saved[4], halo, zero, form
    )
    pins = []
    if direct:
        shares.start("taps", taps_t, taps_s)
        shares.start("last", last_t, last_s)
        shares.step("taps", "x")
        shares.step("last", "z")
        pins = shares.own_part("taps", "last")
    gmf, first_t, first_s, sum_second = run_third(
        *every, back, core, gms, halo_back, zero, taps_full, saved, form, pins
    )
    half = (cnt[1] + 1) // 2
    one = (perm, nval, jnp.stack([start, half, half]))
    rest = (perm, nval, jnp.stack([half, cnt[1], steps]))
    if direct:
        shares.hold(["taps", "last"], gmf)
        shares.start("first", first_t, first_s)
        shares.step("taps", "z")
        shares.step("last", "x", "y")
        pins = shares.own_part("taps", "last")
    part = run_spread(*one, cot, gmf, *saved[1:4], w_full, -(-total // 2), (), pins)
    if direct:
        shares.hold(["first"], part[1])
        shares.step("first", "x", "y")
        pins = shares.own_part("first")
    gin, sum_first = run_spread(*rest, cot, gmf, *saved[1:4], w_full, total, part, pins)

    def column_sums(v):
        return jnp.sum(v.reshape(-1, 8, v.shape[-1]), axis=1)

    sum_first, sum_second, sum_third = (column_sums(v) for v in (sum_first, sum_second, sum_third))
    norms = jnp.concatenate([sum_first, sum_second[:2], sum_third[:2]], axis=1) / vecs[:1]
    biases = jnp.concatenate([sum_out[:1], sum_second[2:], sum_third[2:]], axis=1)
    sums = jnp.concatenate([norms, biases])
    if direct:
        shares.hold(["taps", "last", "first"], sum_first)
        sums = reduce_small(sums, shares.sizes, shares.own)
        shares.step("first", "z")
        grad_taps, grad_last = shares.finish_taps(), shares.finish("last").T
        grad_first = shares.finish("first")
    else:
        grad_taps, grad_last, grad_first, sums = reduce_plainly(taps_t, last_t, first_t, sums)
    return (
        out.reshape(inputs.shape),
        gin.reshape(inputs.shape),
        grad_first,
        grad_taps,
        grad_last,
        sums[0],
        sums[1:],
    )


def solution(mesh):
    placed = (
        P(None, "batch", "seq", None),
        P(None, "batch", "seq", None),
        P(None, "batch"),
        P(("batch", "seq"), None),
        P(None, "batch", "seq"),
        P(None, ("batch", "seq")),
        P(("batch", "seq")),
        P(None, ("batch", "seq")),
    )
    return jax.shard_map(
        shards,
        mesh=mesh,
        in_specs=placed,
        out_specs=(
            P(None, "batch", "seq", None),
            P(None, "batch", "seq", None),
            P(("batch", "seq"), None),
            P(None, "batch", "seq"),
            P(None, ("batch", "seq")),
            P(("batch", "seq")),
            P(None, ("batch", "seq")),
        ),
        check_vma=False,
    )
```

time: 839 us -> 415 us (0.49)
  waiting for transfers between devices: 552 us -> 48.8 us
  starting transfers between devices: 0.24 us -> 98.5 us
  local copies, waits for them, and re-layouts: 65.5 us -> 12 us
  Pallas kernels: 182 us -> 221 us
  between operations: 15.8 us -> 3 us
    unnamed x9 -> x0, waiting for transfers between devices: 392 us -> none
    all_gather x3 -> x0, waiting for transfers between devices: 125 us -> none  [the longest x1 53.7 us: shards(): early = lax.all_gather(jnp.concatenate([w_first, small]), both, axis=0)]
    ppermute x0 -> x41, starting transfers between devices: none -> 98.1 us  [move(): return lax.ppermute(value, ('batch', 'seq'), pairs)]
    ppermute x0 -> x41, waiting for transfers between devices: none -> 44.6 us  [move(): return lax.ppermute(value, ('batch', 'seq'), pairs)]
    pallas_call x3 -> x9, Pallas kernels: 182 us -> 221 us  [the longest x2 64.2 us: run_second(): pl.pallas_call(functools.partial(second_kernel, T, H, len((*old, *pins)))...]
    ppermute x2, waiting for transfers between devices: 34.2 us -> 4.18 us  [from_neighbours(): return lax.ppermute(rows, 'seq', [(0, 1), (1, 0)])]
    convert_element_type x3 -> x0, local copies, waits for them, and re-layouts: 23 us -> none  [shards(): g_taps = g_taps.astype(BF).reshape(n_batch * n_seq, K, rows_t, cols_t)]
    reshape x3 -> x2, local copies, waits for them, and re-layouts: 19.2 us -> 0.54 us  [the longest x1 0.45 us: finish_taps(): v = v.reshape(-1, y, lanes // y).transpose(1, 0, 2)]
  transfers between devices with their start and end apart: 8 -> 43, of which waited for: 7 -> 15; matrix products, arithmetic and copies ran while one was open for 9% -> 9% of each run, Pallas kernels for 3% -> 49%
where the time goes in v2:
time: 415 us; the launch traced here: 411 us
  Pallas kernels  221 us (53%)
  starting transfers between devices  98.5 us (24%)
  waiting for transfers between devices  48.8 us (12%)
  other arithmetic  28.4 us (7%)
  local copies, waits for them, and re-layouts  12 us (3%)
    ppermute x41, starting transfers between devices, move(): return lax.ppermute(value, ('batch', 'seq'), pairs)  98.1 us
    pallas_call x2, Pallas kernels, run_second(): pl.pallas_call(functools.partial(second_kernel, T, H, len((*old, *pins)))...  64.2 us
    pallas_call x1, Pallas kernels, run_third(): pl.pallas_call(functools.partial(third_kernel, T, H, len(pins), form), gr...  48.5 us
    ppermute x41, waiting for transfers between devices, move(): return lax.ppermute(value, ('batch', 'seq'), pairs)  44.6 us
    pallas_call x1, Pallas kernels, run_weights(): pl.pallas_call(functools.partial(weights_kernel, T, H, form), grid_spec=g...  37.4 us
    pallas_call x2, Pallas kernels, run_spread(): pl.pallas_call(functools.partial(spread_kernel, len(old), len((*old, *pin...  30.7 us
    pallas_call x1, Pallas kernels, run_first(): pl.pallas_call(functools.partial(first_kernel, few), grid_spec=grid, out_...  29.7 us
    convert_element_type x4, other arithmetic, piece(): return total.astype(kind if any(off) else F32)  10 us
  transfers between devices with their start and end apart: 43, of which 15 were waited for; matrix products, arithmetic and copies ran while one was open for 9% of the time, Pallas kernels for 49%

profile of v2, /device:TPU:0, one launch (start us, length us, event | category | flops | bytes accessed | tf_op | source)
XLA Modules:
  0.0 411.5 jit_solution(16959920583760090413)
XLA Ops:
  2.2 3.1 collective-permute-start
  5.3 2.6 collective-permute-start.1
  17.8 2.9 collective-permute-start.9
  23.7 2.4 collective-permute-done.7
  26.1 2.4 collective-permute-start.5
  28.7 3.5 collective-permute-done.8
  41.5 9.4 %collective-permute-done.11 = bf16[4,144,640]{2,1,0:T(8,128)(2,1)S(1)} collective-permute-done((bf16[4,144,640]{2,1,0:T(8,128)(2,1)S(1)}, bf16[4,144,640]{2,1,0:T(8,128)(2,1)S(1)}, u32[]{:S(2)}, u32[]{:S(2)}) %collective-permute-start.11) | collective-permute-done | bytes 737312 | tf_op jit(solution)/shard_map/ppermute | solution.py:699
  50.9 2.5 collective-permute-done.12
  53.4 13.5 %collective-permute-done.13 = bf16[4,144,640]{2,1,0:T(8,128)(2,1)} collective-permute-done((bf16[4,144,640]{2,1,0:T(8,128)(2,1)S(1)}, bf16[4,144,640]{2,1,0:T(8,128)(2,1)}, u32[]{:S(2)}, u32[]{:S(2)}) %collective-permute-start.13) | collective-permute-done | bytes 737312 | tf_op jit(solution)/shard_map/ppermute | solution.py:699
  69.4 3.0 early.1
  72.4 29.7 %first.1 = (bf16[4608,1280]{1,0:T(8,128)(2,1)}, bf16[4608,1280]{1,0:T(8,128)(2,1)}, bf16[4608,1280]{1,0:T(8,128)(2,1)}, f32[4608,128]{1,0:T(8,128)}, bf16[4608,6...) custom-call(s32[32]{0:T(128)} %get-tuple-element.155.perm, ...), custom_call_target="tpu_custom_call" | custom-call | flops 27000000512 | bytes 1048576 | tf_op jit(solution)/shard_map/first/pallas_call | solution.py:185
  102.2 7.2 %late.1 = (bf16[3200,640]{1,0:T(8,128)(2,1)}, bf16[1280,640]{1,0:T(8,128)(2,1)}) custom-call(s32[16]{0:T(128)} %add.1459.at, s32[1]{0:T(128)} %bitcast.20.core, bf16[16,144,640]{2,1,0:T(8,128)(2,1)} %bitcast.197, bf16[16,144,640]{2,1,0:T(8,128)(2,1)} %collective-permute-done.14.other), custom_call_target="tpu_custom_call" | custom-call | flops 6300000256 | bytes 1048576 | tf_op jit(solution)/shard_map/late/pallas_call | solution.py:858
  110.0 47.0 %second.2 = (bf16[32,128,1280]{2,1,0:T(8,128)(2,1)}, bf16[4608,640]{1,0:T(8,128)(2,1)}, bf16[4608,640]{1,0:T(8,128)(2,1)}, bf16[4608,1280]{1,0:T(8,128)(2,1)}, f32[24,640]{1,0:T(8,128)}) custom-call(s32[32]{0:T(128)} %get-tuple-element.155.perm, s32[32]{0:T(128)} %get-tuple-element.150.nval, s32[3]{0:T(128)} %pad_add_fusion.4.span, s32[160]{0:T(256)} %reshape.1070.tab, ...), custom_call_target="tpu_custom_call" | custom-call | flops 35999997952 | bytes 1048576 | tf_op jit(solution)/shard_map/second/pallas_call | solution.py:360
  157.1 4.2 %collective-permute-done.10.refs_9_.refs_4_ = bf16[2048,640]{1,0:T(8,128)(2,1)S(1)} collective-permute-done((bf16[2048,640]{1,0:T(8,128)(2,1)}, bf16[2048,640]{1,0:T(8,128)(2,1)S(1)}, u32[]{:S(2)}, u32[]{:S(2)}) %collective-permute-start.10) | collective-permute-done | bytes 2621472 | tf_op jit(solution)/shard_map/ppermute | solution.py:1010
  162.8 17.1 %second.3 = (bf16[32,128,1280]{2,1,0:T(8,128)(2,1)}, bf16[4608,640]{1,0:T(8,128)(2,1)}, bf16[4608,640]{1,0:T(8,128)(2,1)}, bf16[4608,1280]{1,0:T(8,128)(2,1)}, f...) custom-call(s32[32]{0:T(128)} %get-tuple-element.155.perm, ...), custom_call_target="tpu_custom_call", output_to_operand_aliasing={{0}: (18, {}), {1}: (19, {}), {2}: (20, {}), {3}: (21, {})} | custom-call | flops 35999997952 | bytes 1048576 | tf_op jit(solution)/shard_map/second/pallas_call | solution.py:360
  180.3 37.4 %weights.1 = (f32[2,4,5,40,640]{4,3,2,1,0:T(8,128)}, bf16[2,4,5,40,640]{4,3,2,1,0:T(8,128)(2,1)}, f32[4,4,40,640]{3,2,1,0:T(8,128)}, bf16[4,4,40,640]{3,2,1,0:T(8,128)(2,1)}, f32[8,1280]{1,0:T(8,128)}) custom-call(s32[32]{0:T(128)} %get-tuple-element.155.perm, s32[32]{0:T(128)} %get-tuple-element.150.nval, s32[3]{0:T(128)} %pad_add_fusion.5.span, ...), custom_call_target="tpu_custom_call" | custom-call | flops 35999997952 | bytes 1048576 | tf_op jit(solution)/shard_map/weights/pallas_call | solution.py:480
  217.6 6.8 %collective-permute-start.16 = (bf16[2,4,5,40,640]{4,3,2,1,0:T(8,128)(2,1)}, bf16[2,4,5,40,640]{4,3,2,1,0:T(8,128)(2,1)S(1)}, u32[]{:S(2)}, u32[]{:S(2)}) collective-permute-start(bf16[2,4,5,40,640]{4,3,2,1,0:T(8,128)(2,1)} %get-tuple-element.100), channel_id=1, source_target_pairs={{0,2},{1,3},{2,0},{3,1},{4,6},{5,7},{6,4},{7,5},{8,10},{9,11},{10,... | collective-permute-start | bytes 6144008 | tf_op jit(solution)/shard_map/ppermute | solution.py:699
  232.0 9.2 %collective-permute-start.19 = (bf16[4,40,640]{2,1,0:T(8,128)(2,1)}, bf16[4,40,640]{2,1,0:T(8,128)(2,1)}, u32[]{:S(2)}, u32[]{:S(2)}) collective-permute-start(bf16[4,40,640]{2,1,0:T(8,128)(2,1)} %get-tuple-element.171), channel_id=1, source_target_pairs={{0,8},{1,9},{2,10},{3,11},{4,12},{5,13},{6,14},{7,15},{8,16},{9,17... | collective-permute-start | bytes 614408 | tf_op jit(solution)/shard_map/ppermute | solution.py:699
  241.1 2.5 collective-permute-start.21
  243.6 4.3 %fusion = (bf16[4,5,40,640]{3,2,1,0:T(8,128)(2,1)}, f32[4,5,40,640]{3,2,1,0:T(8,128)}) fusion(f32[2,4,5,40,640]{4,3,2,1,0:T(8,128)} %get-tuple-element.99, s32[]{:T(128)S(6)} %select_n.933, bf16[2,4,5,40,640]{4,3,2,1,0:T(8,128)(2,1)S(1)} %collective-permute-done.16, s32[]{:T(128)S(6)} %select_n.929), kind=kLoop, calls=%fused_computation.4 | loop fusion | flops 2560000 | bytes 9216008 | tf_op jit(solution)/shard_map/convert_element_type | solution.py:726
  247.9 15.3 %collective-permute-start.18 = (bf16[4,5,40,640]{3,2,1,0:T(8,128)(2,1)}, bf16[4,5,40,640]{3,2,1,0:T(8,128)(2,1)S(1)}, u32[]{:S(2)}, u32[]{:S(2)}) collective-permute-start(bf16[4,5,40,640]{3,2,1,0:T(8,128)(2,1)} %get-tuple-element.159), channel_id=1, source_target_pairs={{0,4},{1,5},{2,6},{3,7},{4,0},{5,1},{6,2},{7,3},{8,12},{9,13},{10,... | collective-permute-start | bytes 3072008 | tf_op jit(solution)/shard_map/ppermute | solution.py:699
  263.2 48.5 %third.1 = (bf16[4608,640]{1,0:T(8,128)(2,1)}, f32[4,4,40,640]{3,2,1,0:T(8,128)}, bf16[4,4,40,640]{3,2,1,0:T(8,128)(2,1)}, f32[24,640]{1,0:T(8,128)}) custom-call(s32[32]{0:T(128)} %get-tuple-element.155.perm, s32[32]{0:T(128)} %get-tuple-element.150.nval, s32[3]{0:T(128)} %pad_add_fusion.5.span, s32[160]{0:T(256)} %reshape.1079.tab, s32[1]{0:T(128)} %bitcast.20.core, ...), custom_call_target="tpu_custom_call" | custom-call | flops 35999997952 | bytes 1048576 | tf_op jit(solution)/shard_map/third/pallas_call | solution.py:578
  315.9 6.3 %collective-permute-start.23 = (bf16[5,40,640]{2,1,0:T(8,128)(2,1)}, bf16[5,40,640]{2,1,0:T(8,128)(2,1)S(1)}, u32[]{:S(2)}, u32[]{:S(2)}) collective-permute-start(bf16[5,40,640]{2,1,0:T(8,128)(2,1)} %get-tuple-element.163), channel_id=1, source_target_pairs={{0,8},{1,9},{2,10},{3,11},{4,12},{5,13},{6,14},{7,15},{8,16},{9,17... | collective-permute-start | bytes 768008 | tf_op jit(solution)/shard_map/ppermute | solution.py:699
  322.2 14.3 %spread.2 = (bf16[32,128,1280]{2,1,0:T(8,128)(2,1)}, f32[16,1280]{1,0:T(8,128)}) custom-call(s32[32]{0:T(128)} %get-tuple-element.155.perm, s32[32]{0:T(128)} %get-tuple-element.150.nval, s32[3]{0:T(128)} %get-tuple-element.216.span, bf16[32,128,1280]{2,1,0:T(8,128)(2,1)} %bitcast.187, bf16[32,128,1280]{2,1,0:T(8,128)(2,1)} %bitcast.188, ...), custom_call_target="tpu_custom_call" | custom-call | flops 10800000000 | bytes 1048576 | tf_op jit(solution)/shard_map/spread/pallas_call | solution.py:657
  338.7 16.4 %spread.3 = (bf16[32,128,1280]{2,1,0:T(8,128)(2,1)}, f32[16,1280]{1,0:T(8,128)}) custom-call(s32[32]{0:T(128)} %get-tuple-element.155.perm, s32[32]{0:T(128)} %get-tuple-element.150.nval, s32[3]{0:T(128)} %get-tuple-element.215.span, bf16[32,128,1280]{2,1,0:T(8,128)(2,1)} %bitcast.191, ...), custom_call_target="tpu_custom_call", output_to_operand_aliasing={{0}: (12, {})} | custom-call | flops 10800000000 | bytes 1048576 | tf_op jit(solution)/shard_map/spread/pallas_call | solution.py:657
  359.7 8.2 %collective-permute-start.38 = (f32[4,3,80]{2,1,0:T(4,128)S(1)}, f32[4,3,80]{2,1,0:T(4,128)S(1)}, u32[]{:S(2)}, u32[]{:S(2)}) collective-permute-start(f32[4,3,80]{2,1,0:T(4,128)S(1)} %bitcast_add_fusion.3), channel_id=1, source_target_pairs={{0,4},{1,5},{2,6},{3,7},{4,0},{5,1},{6,2},{7,3},{8,12},{9,13},{10,... | collective-permute-start | bytes 11528 | tf_op jit(solution)/shard_map/ppermute | solution.py:699
  371.6 3.7 collective-permute-start.42
  381.2 3.8 collective-permute-start.25
  387.5 7.3 %collective-permute-start.30 = (bf16[4,40,640]{2,1,0:T(8,128)(2,1)S(1)}, bf16[4,40,640]{2,1,0:T(8,128)(2,1)S(1)}, u32[]{:S(2)}, u32[]{:S(2)}) collective-permute-start(bf16[4,40,640]{2,1,0:T(8,128)(2,1)S(1)} %get-tuple-element.166), channel_id=1, source_target_pairs={{0,4},{1,5},{2,6},{3,7},{4,0},{5,1},{6,2},{7,3},{8,12},{9,13},{10,... | collective-permute-start | bytes 614408 | tf_op jit(solution)/shard_map/ppermute | solution.py:699
  395.3 3.2 collective-permute-done.30
  398.5 2.9 collective-permute-done.31
  403.9 3.3 collective-permute-start.34
  (202 shorter events, 64.6 us)
Async XLA Ops:
  2.2 14.4 %collective-permute-start = (bf16[48,640]{1,0:T(8,128)(2,1)S(1)}, bf16[48,640]{1,0:T(8,128)(2,1)S(1)}, u32[]{:S(2)}, u32[]{:S(2)}) collective-permute-start(bf16[48,640]{1,0:T(8,128)(2,1)S(1)} %get-tuple-element.183), channel_id=1, source_target_pairs={{0,8},{1,9},{2,10},{3,11},{4,12},{5,13},{6,14},{7,15},{8,16},{9,17... | collective-permute-start | bytes 184328 | tf_op jit(solution)/shard_map/ppermute | solution.py:699
  5.3 11.3 %collective-permute-start.1 = (bf16[48,640]{1,0:T(8,128)(2,1)S(1)}, bf16[48,640]{1,0:T(8,128)(2,1)S(1)}, u32[]{:S(2)}, u32[]{:S(2)}) collective-permute-start(bf16[48,640]{1,0:T(8,128)(2,1)S(1)} %get-tuple-element.183), channel_id=1, source_target_pairs={{0,16},{1,17},{2,18},{3,19},{4,20},{5,21},{6,22},{7,23},{8,24},{9,... | collective-permute-start | bytes 184328 | tf_op jit(solution)/shard_map/ppermute | solution.py:699
  7.9 8.7 %collective-permute-start.2 = (bf16[48,640]{1,0:T(8,128)(2,1)S(1)}, bf16[48,640]{1,0:T(8,128)(2,1)S(1)}, u32[]{:S(2)}, u32[]{:S(2)}) collective-permute-start(bf16[48,640]{1,0:T(8,128)(2,1)S(1)} %get-tuple-element.183), channel_id=1, source_target_pairs={{0,24},{1,25},{2,26},{3,27},{4,28},{5,29},{6,30},{7,31},{8,0},{9,1... | collective-permute-start | bytes 184328 | tf_op jit(solution)/shard_map/ppermute | solution.py:699
  16.7 9.5 %collective-permute-start.7 = (bf16[144,640]{1,0:T(8,128)(2,1)S(1)}, bf16[144,640]{1,0:T(8,128)(2,1)S(1)}, u32[]{:S(2)}, u32[]{:S(2)}) collective-permute-start(bf16[144,640]{1,0:T(8,128)(2,1)S(1)} %fusion.14), channel_id=1, source_target_pairs={{0,8},{1,9},{2,10},{3,11},{4,12},{5,13},{6,14},{7,15},{8,16},{9,17... | collective-permute-start | bytes 552968 | tf_op jit(solution)/shard_map/ppermute | solution.py:699
  17.4 14.7 %collective-permute-start.8 = (bf16[144,640]{1,0:T(8,128)(2,1)S(1)}, bf16[144,640]{1,0:T(8,128)(2,1)S(1)}, u32[]{:S(2)}, u32[]{:S(2)}) collective-permute-start(bf16[144,640]{1,0:T(8,128)(2,1)S(1)} %fusion.14), channel_id=1, source_target_pairs={{0,16},{1,17},{2,18},{3,19},{4,20},{5,21},{6,22},{7,23},{8,24},{9,... | collective-permute-start | bytes 552968 | tf_op jit(solution)/shard_map/ppermute | solution.py:699
  17.8 14.3 %collective-permute-start.9 = (bf16[144,640]{1,0:T(8,128)(2,1)S(1)}, bf16[144,640]{1,0:T(8,128)(2,1)S(1)}, u32[]{:S(2)}, u32[]{:S(2)}) collective-permute-start(bf16[144,640]{1,0:T(8,128)(2,1)S(1)} %fusion.14), channel_id=1, source_target_pairs={{0,24},{1,25},{2,26},{3,27},{4,28},{5,29},{6,30},{7,31},{8,0},{9,1... | collective-permute-start | bytes 552968 | tf_op jit(solution)/shard_map/ppermute | solution.py:699
  20.7 14.7 %collective-permute-start.3 = (bf16[4,48,640]{2,1,0:T(8,128)(2,1)S(1)}, bf16[4,48,640]{2,1,0:T(8,128)(2,1)}, u32[]{:S(2)}, u32[]{:S(2)}) collective-permute-start(bf16[4,48,640]{2,1,0:T(8,128)(2,1)S(1)} %pad_maximum_fusion.3), channel_id=1, source_target_pairs={{0,1},{1,0},{2,3},{3,2},{4,5},{5,4},{6,7},{7,6},{8,9},{9,8},{10,11... | collective-permute-start | bytes 737288 | tf_op jit(solution)/shard_map/ppermute | solution.py:699
  22.2 13.6 %collective-permute-start.4 = (bf16[4,48,640]{2,1,0:T(8,128)(2,1)S(1)}, bf16[4,48,640]{2,1,0:T(8,128)(2,1)}, u32[]{:S(2)}, u32[]{:S(2)}) collective-permute-start(bf16[4,48,640]{2,1,0:T(8,128)(2,1)S(1)} %pad_maximum_fusion.3), channel_id=1, source_target_pairs={{0,4},{1,5},{2,6},{3,7},{4,0},{5,1},{6,2},{7,3},{8,12},{9,13},{10,... | collective-permute-start | bytes 737288 | tf_op jit(solution)/shard_map/ppermute | solution.py:699
  26.1 9.7 %collective-permute-start.5 = (bf16[4,48,640]{2,1,0:T(8,128)(2,1)S(1)}, bf16[4,48,640]{2,1,0:T(8,128)(2,1)}, u32[]{:S(2)}, u32[]{:S(2)}) collective-permute-start(bf16[4,48,640]{2,1,0:T(8,128)(2,1)S(1)} %pad_maximum_fusion.3), channel_id=1, source_target_pairs={{0,5},{1,4},{2,7},{3,6},{4,1},{5,0},{6,3},{7,2},{8,13},{9,12},{10,... | collective-permute-start | bytes 737288 | tf_op jit(solution)/shard_map/ppermute | solution.py:699
  32.3 18.6 %collective-permute-start.11 = (bf16[4,144,640]{2,1,0:T(8,128)(2,1)S(1)}, bf16[4,144,640]{2,1,0:T(8,128)(2,1)S(1)}, u32[]{:S(2)}, u32[]{:S(2)}) collective-permute-start(bf16[4,144,640]{2,1,0:T(8,128)(2,1)S(1)} %get-tuple-element.181.held), channel_id=1, source_target_pairs={{0,1},{1,0},{2,3},{3,2},{4,5},{5,4},{6,7},{7,6},{8,9},{9,8},{10,11... | collective-permute-start | bytes 2211848 | tf_op jit(solution)/shard_map/ppermute | solution.py:699
  33.9 19.5 %collective-permute-start.12 = (bf16[4,144,640]{2,1,0:T(8,128)(2,1)S(1)}, bf16[4,144,640]{2,1,0:T(8,128)(2,1)}, u32[]{:S(2)}, u32[]{:S(2)}) collective-permute-start(bf16[4,144,640]{2,1,0:T(8,128)(2,1)S(1)} %get-tuple-element.181.held), channel_id=1, source_target_pairs={{0,4},{1,5},{2,6},{3,7},{4,0},{5,1},{6,2},{7,3},{8,12},{9,13},{10,... | collective-permute-start | bytes 2211848 | tf_op jit(solution)/shard_map/ppermute | solution.py:699
  35.4 31.5 %collective-permute-start.13 = (bf16[4,144,640]{2,1,0:T(8,128)(2,1)S(1)}, bf16[4,144,640]{2,1,0:T(8,128)(2,1)}, u32[]{:S(2)}, u32[]{:S(2)}) collective-permute-start(bf16[4,144,640]{2,1,0:T(8,128)(2,1)S(1)} %get-tuple-element.181.held), channel_id=1, source_target_pairs={{0,5},{1,4},{2,7},{3,6},{4,1},{5,0},{6,3},{7,2},{8,13},{9,12},{10,... | collective-permute-start | bytes 2211848 | tf_op jit(solution)/shard_map/ppermute | solution.py:699
  37.2 32.2 %collective-permute-start.6 = (bf16[16,48,640]{2,1,0:T(8,128)(2,1)S(1)}, bf16[16,48,640]{2,1,0:T(8,128)(2,1)}, u32[]{:S(2)}, u32[]{:S(2)}) collective-permute-start(bf16[16,48,640]{2,1,0:T(8,128)(2,1)S(1)} %bitcast.198), channel_id=1, source_target_pairs={{0,2},{1,3},{2,0},{3,1},{4,6},{5,7},{6,4},{7,5},{8,10},{9,11},{10,... | collective-permute-start | bytes 2949128 | tf_op jit(solution)/shard_map/ppermute | solution.py:699
  68.5 33.6 %collective-permute-start.14 = (bf16[16,144,640]{2,1,0:T(8,128)(2,1)S(1)}, bf16[16,144,640]{2,1,0:T(8,128)(2,1)}, u32[]{:S(2)}, u32[]{:S(2)}) collective-permute-start(bf16[16,144,640]{2,1,0:T(8,128)(2,1)S(1)} %bitcast.196), channel_id=1, source_target_pairs={{0,2},{1,3},{2,0},{3,1},{4,6},{5,7},{6,4},{7,5},{8,10},{9,11},{10,... | collective-permute-start | bytes 8847368 | tf_op jit(solution)/shard_map/ppermute | solution.py:699
  102.1 59.2 %collective-permute-start.10 = (bf16[2048,640]{1,0:T(8,128)(2,1)}, bf16[2048,640]{1,0:T(8,128)(2,1)S(1)}, u32[]{:S(2)}, u32[]{:S(2)}) collective-permute-start(bf16[2048,640]{1,0:T(8,128)(2,1)} %get-tuple-element.83), channel_id=1, source_target_pairs={{0,1},{1,0},{2,3},{3,2},{4,5},{5,4},{6,7},{7,6},{8,9},{9,8},{10,11... | collective-permute-start | bytes 7864328 | tf_op jit(solution)/shard_map/ppermute | solution.py:1010
  179.9 83.3 %collective-permute-start.15 = (bf16[2048,640]{1,0:T(8,128)(2,1)}, bf16[2048,640]{1,0:T(8,128)(2,1)}, u32[]{:S(2)}, u32[]{:S(2)}) collective-permute-start(bf16[2048,640]{1,0:T(8,128)(2,1)} %get-tuple-element.92), channel_id=1, source_target_pairs={{0,1},{1,0},{2,3},{3,2},{4,5},{5,4},{6,7},{7,6},{8,9},{9,8},{10,11... | collective-permute-start | bytes 7864328 | tf_op jit(solution)/shard_map/ppermute | solution.py:1010
  217.6 25.9 %collective-permute-start.16 = (bf16[2,4,5,40,640]{4,3,2,1,0:T(8,128)(2,1)}, bf16[2,4,5,40,640]{4,3,2,1,0:T(8,128)(2,1)S(1)}, u32[]{:S(2)}, u32[]{:S(2)}) collective-permute-start(bf16[2,4,5,40,640]{4,3,2,1,0:T(8,128)(2,1)} %get-tuple-element.100), channel_id=1, source_target_pairs={{0,2},{1,3},{2,0},{3,1},{4,6},{5,7},{6,4},{7,5},{8,10},{9,11},{10,... | collective-permute-start | bytes 6144008 | tf_op jit(solution)/shard_map/ppermute | solution.py:699
  232.0 80.9 %collective-permute-start.19 = (bf16[4,40,640]{2,1,0:T(8,128)(2,1)}, bf16[4,40,640]{2,1,0:T(8,128)(2,1)}, u32[]{:S(2)}, u32[]{:S(2)}) collective-permute-start(bf16[4,40,640]{2,1,0:T(8,128)(2,1)} %get-tuple-element.171), channel_id=1, source_target_pairs={{0,8},{1,9},{2,10},{3,11},{4,12},{5,13},{6,14},{7,15},{8,16},{9,17... | collective-permute-start | bytes 614408 | tf_op jit(solution)/shard_map/ppermute | solution.py:699
  241.1 71.7 %collective-permute-start.20 = (bf16[4,40,640]{2,1,0:T(8,128)(2,1)}, bf16[4,40,640]{2,1,0:T(8,128)(2,1)}, u32[]{:S(2)}, u32[]{:S(2)}) collective-permute-start(bf16[4,40,640]{2,1,0:T(8,128)(2,1)} %get-tuple-element.170), channel_id=1, source_target_pairs={{0,16},{1,17},{2,18},{3,19},{4,20},{5,21},{6,22},{7,23},{8,24},{9,... | collective-permute-start | bytes 614408 | tf_op jit(solution)/shard_map/ppermute | solution.py:699
  241.1 71.7 %collective-permute-start.21 = (bf16[4,40,640]{2,1,0:T(8,128)(2,1)}, bf16[4,40,640]{2,1,0:T(8,128)(2,1)}, u32[]{:S(2)}, u32[]{:S(2)}) collective-permute-start(bf16[4,40,640]{2,1,0:T(8,128)(2,1)} %get-tuple-element.169), channel_id=1, source_target_pairs={{0,24},{1,25},{2,26},{3,27},{4,28},{5,29},{6,30},{7,31},{8,0},{9,1... | collective-permute-start | bytes 614408 | tf_op jit(solution)/shard_map/ppermute | solution.py:699
  247.9 65.0 %collective-permute-start.18 = (bf16[4,5,40,640]{3,2,1,0:T(8,128)(2,1)}, bf16[4,5,40,640]{3,2,1,0:T(8,128)(2,1)S(1)}, u32[]{:S(2)}, u32[]{:S(2)}) collective-permute-start(bf16[4,5,40,640]{3,2,1,0:T(8,128)(2,1)} %get-tuple-element.159), channel_id=1, source_target_pairs={{0,4},{1,5},{2,6},{3,7},{4,0},{5,1},{6,2},{7,3},{8,12},{9,13},{10,... | collective-permute-start | bytes 3072008 | tf_op jit(solution)/shard_map/ppermute | solution.py:699
  312.6 23.9 %collective-permute-start.22 = (bf16[4,4,40,640]{3,2,1,0:T(8,128)(2,1)}, bf16[4,4,40,640]{3,2,1,0:T(8,128)(2,1)}, u32[]{:S(2)}, u32[]{:S(2)}) collective-permute-start(bf16[4,4,40,640]{3,2,1,0:T(8,128)(2,1)} %get-tuple-element.116), channel_id=1, source_target_pairs={{0,2},{1,3},{2,0},{3,1},{4,6},{5,7},{6,4},{7,5},{8,10},{9,11},{10,... | collective-permute-start | bytes 2457608 | tf_op jit(solution)/shard_map/ppermute | solution.py:699
  314.7 61.2 %collective-permute-start.26 = (bf16[40,640]{1,0:T(8,128)(2,1)}, bf16[40,640]{1,0:T(8,128)(2,1)}, u32[]{:S(2)}, u32[]{:S(2)}) collective-permute-start(bf16[40,640]{1,0:T(8,128)(2,1)} %get-tuple-element.178), channel_id=1, source_target_pairs={{0,1},{1,0},{2,3},{3,2},{4,5},{5,4},{6,7},{7,6},{8,9},{9,8},{10,11... | collective-permute-start | bytes 153608 | tf_op jit(solution)/shard_map/ppermute | solution.py:699
  315.9 78.9 %collective-permute-start.23 = (bf16[5,40,640]{2,1,0:T(8,128)(2,1)}, bf16[5,40,640]{2,1,0:T(8,128)(2,1)S(1)}, u32[]{:S(2)}, u32[]{:S(2)}) collective-permute-start(bf16[5,40,640]{2,1,0:T(8,128)(2,1)} %get-tuple-element.163), channel_id=1, source_target_pairs={{0,8},{1,9},{2,10},{3,11},{4,12},{5,13},{6,14},{7,15},{8,16},{9,17... | collective-permute-start | bytes 768008 | tf_op jit(solution)/shard_map/ppermute | solution.py:699
  357.7 11.7 %collective-permute-start.39 = (f32[4,3,80]{2,1,0:T(4,128)S(1)}, f32[4,3,80]{2,1,0:T(4,128)S(1)}, u32[]{:S(2)}, u32[]{:S(2)}) collective-permute-start(f32[4,3,80]{2,1,0:T(4,128)S(1)} %bitcast_add_fusion.2), channel_id=1, source_target_pairs={{0,5},{1,4},{2,7},{3,6},{4,1},{5,0},{6,3},{7,2},{8,13},{9,12},{10,... | collective-permute-start | bytes 11528 | tf_op jit(solution)/shard_map/ppermute | solution.py:699
  359.7 9.8 %collective-permute-start.38 = (f32[4,3,80]{2,1,0:T(4,128)S(1)}, f32[4,3,80]{2,1,0:T(4,128)S(1)}, u32[]{:S(2)}, u32[]{:S(2)}) collective-permute-start(f32[4,3,80]{2,1,0:T(4,128)S(1)} %bitcast_add_fusion.3), channel_id=1, source_target_pairs={{0,4},{1,5},{2,6},{3,7},{4,0},{5,1},{6,2},{7,3},{8,12},{9,13},{10,... | collective-permute-start | bytes 11528 | tf_op jit(solution)/shard_map/ppermute | solution.py:699
  376.0 9.6 %collective-permute-start.27 = (bf16[40,640]{1,0:T(8,128)(2,1)S(1)}, bf16[40,640]{1,0:T(8,128)(2,1)S(1)}, u32[]{:S(2)}, u32[]{:S(2)}) collective-permute-start(bf16[40,640]{1,0:T(8,128)(2,1)S(1)} %copy-done.13), channel_id=1, source_target_pairs={{0,4},{1,5},{2,6},{3,7},{4,0},{5,1},{6,2},{7,3},{8,12},{9,13},{10,... | collective-permute-start | bytes 153608 | tf_op jit(solution)/shard_map/ppermute | solution.py:699
  377.4 10.2 %collective-permute-start.28 = (bf16[40,640]{1,0:T(8,128)(2,1)S(1)}, bf16[40,640]{1,0:T(8,128)(2,1)S(1)}, u32[]{:S(2)}, u32[]{:S(2)}) collective-permute-start(bf16[40,640]{1,0:T(8,128)(2,1)S(1)} %copy-done.12), channel_id=1, source_target_pairs={{0,5},{1,4},{2,7},{3,6},{4,1},{5,0},{6,3},{7,2},{8,13},{9,12},{10,... | collective-permute-start | bytes 153608 | tf_op jit(solution)/shard_map/ppermute | solution.py:699
  380.7 14.6 %collective-permute-start.24 = (bf16[5,40,640]{2,1,0:T(8,128)(2,1)S(1)}, bf16[5,40,640]{2,1,0:T(8,128)(2,1)S(1)}, u32[]{:S(2)}, u32[]{:S(2)}) collective-permute-start(bf16[5,40,640]{2,1,0:T(8,128)(2,1)S(1)} %copy-done.9), channel_id=1, source_target_pairs={{0,16},{1,17},{2,18},{3,19},{4,20},{5,21},{6,22},{7,23},{8,24},{9,... | collective-permute-start | bytes 768008 | tf_op jit(solution)/shard_map/ppermute | solution.py:699
  381.2 14.1 %collective-permute-start.25 = (bf16[5,40,640]{2,1,0:T(8,128)(2,1)S(1)}, bf16[5,40,640]{2,1,0:T(8,128)(2,1)S(1)}, u32[]{:S(2)}, u32[]{:S(2)}) collective-permute-start(bf16[5,40,640]{2,1,0:T(8,128)(2,1)S(1)} %get-tuple-element.161), channel_id=1, source_target_pairs={{0,24},{1,25},{2,26},{3,27},{4,28},{5,29},{6,30},{7,31},{8,0},{9,1... | collective-permute-start | bytes 768008 | tf_op jit(solution)/shard_map/ppermute | solution.py:699
  385.6 9.7 %collective-permute-start.29 = (bf16[4,40,640]{2,1,0:T(8,128)(2,1)S(1)}, bf16[4,40,640]{2,1,0:T(8,128)(2,1)S(1)}, u32[]{:S(2)}, u32[]{:S(2)}) collective-permute-start(bf16[4,40,640]{2,1,0:T(8,128)(2,1)S(1)} %get-tuple-element.167), channel_id=1, source_target_pairs={{0,1},{1,0},{2,3},{3,2},{4,5},{5,4},{6,7},{7,6},{8,9},{9,8},{10,11... | collective-permute-start | bytes 614408 | tf_op jit(solution)/shard_map/ppermute | solution.py:699
  387.5 11.0 %collective-permute-start.30 = (bf16[4,40,640]{2,1,0:T(8,128)(2,1)S(1)}, bf16[4,40,640]{2,1,0:T(8,128)(2,1)S(1)}, u32[]{:S(2)}, u32[]{:S(2)}) collective-permute-start(bf16[4,40,640]{2,1,0:T(8,128)(2,1)S(1)} %get-tuple-element.166), channel_id=1, source_target_pairs={{0,4},{1,5},{2,6},{3,7},{4,0},{5,1},{6,2},{7,3},{8,12},{9,13},{10,... | collective-permute-start | bytes 614408 | tf_op jit(solution)/shard_map/ppermute | solution.py:699
  (32 other events, 775.2 us)
